TPU v7x, 32 devices: a whole 2x2x4 slice. The times are simulated.
32 devices in a mesh: segment: 4 (over x, core), dp: 8 (over z, y).
Axes of the slice: x: 2, y: 2, z: 4, core: 2. Of those that a mesh axis runs over, the one named last changes fastest.
Arguments:
- images: bfloat16 [8, 14, 14, 384], P('dp'), may hold values from -6 to 6
- cotangent: bfloat16 [2, 8, 14, 14, 384], P(None, 'dp'), may hold values from -6 to 6
- picks: int32 [2, 8], P(None, 'segment'), may hold values from 0 to 47
- section_sizes: int32 [4], P('segment'), may hold values from 1 to 2, 6 in all
- kernels: bfloat16 [8, 48, 25, 384], P('segment'), may hold values from -1.1953125 to 1.1953125
- weights: bfloat16 [8, 48, 384, 384], P('segment', None, 'dp'), may hold values from -0.15625 to 0.15625
- first_moment: float32 [8, 48, 384, 384], P('segment', None, 'dp'), may hold values from -0.006 to 0.006
- second_moment: float32 [8, 48, 384, 384], P('segment', None, 'dp'), may hold values from 1e-08 to 1e-07
Outputs:
- new_weights: bfloat16 [2, 8, 384, 384], P(None, 'segment', 'dp')
- new_first: float32 [2, 8, 384, 384], P(None, 'segment', 'dp')
- new_second: float32 [2, 8, 384, 384], P(None, 'segment', 'dp')
Inputs may be any that keep to these rules, and one draw needn't show every extreme that they name: `section_sizes`: the counts sum to 6, and one of them equals 2.
All inputs are finite; a program needn't handle non-finite values. No bound on the sum of `section_sizes` on one device may be relied on, other than what follows from the above.
Results may differ from a plain program's by a relative error of at most 0.03.
Values may be sent and summed in bfloat16 or wider, within the bound.
A program may use at most 128 MiB of HBM per device.

v0:
```python
import functools

import jax
import jax.numpy as jnp
from jax import lax
from jax.experimental import pallas as pl
from jax.experimental.pallas import tpu as pltpu
from jax.sharding import PartitionSpec as P

first_decay = 0.9
second_decay = 0.999
learn_rate = 0.01
adam_epsilon = 1e-08
first_bias = 1.0 - 0.9**10
second_bias = 1.0 - 0.999**10
MESH = pl.DeviceIdType.MESH
SUB = 8
LANES = 128


def pick_kernel(
    picks_ref, size_ref, k_hbm, w_hbm, m_hbm, v_hbm, k_out, w_out, live_out, m_out, v_out, sem
):
    slots = w_out.shape[1]
    copies = []
    for n in range(2):
        for j in range(slots):
            o = picks_ref[n, j]
            for i, (src, dst) in enumerate(
                ((w_hbm, w_out), (k_hbm, k_out), (m_hbm, m_out), (v_hbm, v_out))
            ):
                copy = pltpu.make_async_copy(src.at[j, o], dst.at[n, j], sem.at[i, n, j])
                copy.start()
                copies.append(copy)
    for copy in copies:
        copy.wait()
    for j in range(slots):
        scale = jnp.where(j < size_ref[0], 1.0, 0.0).astype(jnp.float32)
        for n in range(2):
            live_out[n, j] = (w_out[n, j].astype(jnp.float32) * scale).astype(jnp.bfloat16)


def pick(picks, sizes, kernels, weights, first, second):
    slots, _, taps, width = kernels.shape
    rows = weights.shape[2]
    shape = jax.ShapeDtypeStruct
    vmem = pl.BlockSpec(memory_space=pltpu.VMEM)
    smem = pl.BlockSpec(memory_space=pltpu.SMEM)
    hbm = pl.BlockSpec(memory_space=pl.ANY)
    return pl.pallas_call(
        pick_kernel,
        out_shape=(
            shape((2, slots, taps, width), jnp.bfloat16),
            shape((2, slots, rows, width), jnp.bfloat16),
            shape((2, slots, rows, width), jnp.bfloat16),
            shape((2, slots, rows, width), jnp.float32),
            shape((2, slots, rows, width), jnp.float32),
        ),
        in_specs=[smem, smem, hbm, hbm, hbm, hbm],
        out_specs=(vmem,) * 5,
        scratch_shapes=[pltpu.SemaphoreType.DMA((4, 2, slots))],
        compiler_params=pltpu.CompilerParams(vmem_limit_bytes=16 * 1024 * 1024),
        name="pick_rows",
    )(picks, sizes, kernels, weights, first, second)


def put_shifts(shifted, value, lanes):
    shifted[1, :, :, lanes] = value
    shifted[0, :, :, lanes] = pltpu.roll(value, 1, 1)
    shifted[2, :, :, lanes] = pltpu.roll(value, SUB - 1, 1)


def conv_columns(shifted, taps, side, lanes, emit):
    weights = [taps(t) for t in range(25)]
    loaded = {}

    def cell(sh, r, q):
        if (sh, r, q) not in loaded:
            loaded[sh, r, q] = shifted[sh + 1, r * side + q, :, lanes]
        return loaded[sh, r, q]

    for q in range(side):
        for r in range(2):
            parts = []
            for e in range(-2, 3):
                if not 0 <= q + e < side:
                    continue
                part = None
                for a in range(-2, 3):
                    sh, rr = (r + a) // 2, (r + a) % 2
                    term = weights[(a + 2) * 5 + e + 2] * cell(sh, rr, q + e)
                    part = term if part is None else part + term
                parts.append(part)
            total = parts[0]
            for part in parts[1:]:
                total = total + part
            emit(r, q, total)


def train_kernel(
    segments, dps, side,
    image_ref, cot_ref, k_ref, w_ref,
    g_out,
    x_buf, up_buf, h_buf, act_buf, w_full, g_send, g_recv, shifted, taps_wide,
    joined, w_ssem, w_rsem, g_ssem, g_rsem, x_ssem, x_rsem, d_ssem, d_rsem,
):
    place = lax.axis_index("segment")
    me = lax.axis_index("dp")
    slots = w_ref.shape[1]
    rows = w_ref.shape[2]
    width = w_ref.shape[3]
    cells = x_buf.shape[2]
    tiles = width // LANES
    others = pl.ds(0, dps - 1)
    aligned = rows % 16 == 0

    barrier = pltpu.get_barrier_semaphore()

    def greet(d, carry):
        pl.semaphore_signal(
            barrier, inc=1, device_id={"dp": lax.rem(me + d, dps)}, device_id_type=MESH
        )
        return carry

    lax.fori_loop(1, dps, greet, 0)

    for step in (1, segments - 1):
        pl.semaphore_signal(
            barrier,
            inc=1,
            device_id={"segment": lax.rem(place + step, segments)},
            device_id_type=MESH,
        )

    for n in range(2):
        for j in range(slots):
            w_full[n, j, me] = w_ref[n, j]
            for t in range(25):
                taps_wide[n, j, t] = jnp.broadcast_to(
                    k_ref[n, j, t : t + 1, :].astype(jnp.float32), (SUB, width)
                )

    @pl.when(place == 0)
    def _():
        for n in range(2):
            x_buf[n, 0] = image_ref[...]

    @pl.when(place == segments - 1)
    def _():
        for n in range(2):
            up_buf[n, slots] = cot_ref[n]

    pl.semaphore_wait(barrier, dps + 1)

    for n in range(2):
        for j in range(slots):

            def send_rows(d, carry):
                pltpu.make_async_remote_copy(
                    src_ref=w_ref.at[n, j],
                    dst_ref=w_full.at[n, j, me],
                    send_sem=w_ssem.at[n, j],
                    recv_sem=w_rsem.at[n, j],
                    device_id={"dp": lax.rem(me + d, dps)},
                    device_id_type=MESH,
                ).start()
                return carry

            lax.fori_loop(1, dps, send_rows, 0)

    def x_copy(n):
        return pltpu.make_async_remote_copy(
            src_ref=x_buf.at[n, slots],
            dst_ref=x_buf.at[n, 0],
            send_sem=x_ssem.at[n],
            recv_sem=x_rsem.at[n],
            device_id={"segment": lax.rem(place + 1, segments)},
            device_id_type=MESH,
        )

    def d_copy(n):
        return pltpu.make_async_remote_copy(
            src_ref=up_buf.at[n, 0],
            dst_ref=up_buf.at[n, slots],
            send_sem=d_ssem.at[n],
            recv_sem=d_rsem.at[n],
            device_id={"segment": lax.rem(place + segments - 1, segments)},
            device_id_type=MESH,
        )

    def wait_bytes(ref, sem):
        pltpu.make_async_copy(ref, ref, sem).wait()

    inside = lax.broadcasted_iota(jnp.int32, (SUB, LANES), 0) < side // 2

    def lane_slice(ct):
        return pl.ds(pl.multiple_of(ct * LANES, LANES), LANES)

    def weight_of(n, j):
        if aligned:
            return w_full[n, j].reshape(width, width)
        for k in range(dps):
            joined[k * rows : (k + 1) * rows] = w_full[n, j, k].astype(jnp.float32)
        return joined[...].astype(jnp.bfloat16)

    def store_grad(n, j, grad):
        if aligned:
            g_send[n, j] = grad.astype(jnp.bfloat16).reshape(dps, rows, width)
        else:
            joined[...] = grad
            for k in range(dps):
                g_send[n, j, k] = joined[k * rows : (k + 1) * rows].astype(jnp.bfloat16)

    def slot_forward(n, j):
        def tile(ct, carry):
            lanes = lane_slice(ct)
            value = x_buf[n, j, :, lanes].astype(jnp.float32).reshape(2 * side, SUB, LANES)
            put_shifts(shifted, value, lanes)

            def emit(r, q, u):
                s = 0.5 * jnp.tanh(0.5 * u) + 0.5
                at = r * side + q
                act_buf[n, j, at, :, lanes] = jnp.where(inside, s * (1.0 + u * (1.0 - s)), 0.0)
                shifted[3, at, :, lanes] = jnp.where(inside, u * s, 0.0)

            conv_columns(
                shifted, lambda t: taps_wide[n, j, t, :, lanes], side, lanes, emit
            )
            h_buf[n, j, :, lanes] = (
                shifted[3, :, :, lanes].reshape(cells, LANES).astype(jnp.bfloat16)
            )
            return carry

        lax.fori_loop(0, tiles, tile, 0)

    def forward(n, carry):
        @pl.when(place > 0)
        def _():
            x_copy(n).wait_recv()

        for j in range(slots):
            slot_forward(n, j)
            wait_bytes(w_full.at[n, j, others], w_rsem.at[n, j])

            def project():
                update = jnp.dot(
                    h_buf[n, j], weight_of(n, j), preferred_element_type=jnp.float32
                )
                x_buf[n, j + 1] = (x_buf[n, j].astype(jnp.float32) + update).astype(
                    jnp.bfloat16
                )

            if j + 1 < slots:
                project()
            else:
                pl.when(place < segments - 1)(project)

        @pl.when(place < segments - 1)
        def _():
            x_copy(n).start()

        return carry

    lax.fori_loop(0, 2, forward, 0)

    def backward(n, carry):
        @pl.when(place < segments - 1)
        def _():
            d_copy(n).wait_recv()

        for j in reversed(range(slots)):

            def slot_backward():
                back = lax.dot_general(
                    up_buf[n, j + 1],
                    weight_of(n, j),
                    (((1,), (1,)), ((), ())),
                    preferred_element_type=jnp.float32,
                )
                shifted[3] = back.reshape(2 * side, SUB, width)

                def tile(ct, carry):
                    lanes = lane_slice(ct)
                    put_shifts(shifted, shifted[3, :, :, lanes] * act_buf[n, j, :, :, lanes], lanes)

                    def emit(r, q, total):
                        shifted[3, r * side + q, :, lanes] = total

                    conv_columns(
                        shifted, lambda t: taps_wide[n, j, 24 - t, :, lanes], side, lanes, emit
                    )
                    up_buf[n, j, :, lanes] = (
                        up_buf[n, j + 1, :, lanes].astype(jnp.float32)
                        + jnp.where(
                            inside[None], shifted[3, :, :, lanes], 0.0
                        ).reshape(cells, LANES)
                    ).astype(jnp.bfloat16)
                    return carry

                lax.fori_loop(0, tiles, tile, 0)

            if j > 0:
                slot_backward()
            else:
                pl.when(place > 0)(slot_backward)

        @pl.when(place > 0)
        def _():
            d_copy(n).start()

        for j in reversed(range(slots)):
            grad = lax.dot_general(
                h_buf[n, j],
                up_buf[n, j + 1],
                (((0,), (0,)), ((), ())),
                preferred_element_type=jnp.float32,
            )
            store_grad(n, j, grad)

            def send_grad(d, carry):
                owner = lax.rem(me + d, dps)
                pltpu.make_async_remote_copy(
                    src_ref=g_send.at[n, j, owner],
                    dst_ref=g_recv.at[n, j, d - 1],
                    send_sem=g_ssem.at[n, j],
                    recv_sem=g_rsem.at[n, j],
                    device_id={"dp": owner},
                    device_id_type=MESH,
                ).start()
                return carry

            lax.fori_loop(1, dps, send_grad, 0)
        return carry

    lax.fori_loop(0, 2, backward, 0)

    for n in range(2):
        for j in reversed(range(slots)):
            wait_bytes(g_recv.at[n, j], g_rsem.at[n, j])

            def add(d, total):
                return total + g_recv[n, j, d].astype(jnp.float32)

            g_out[n, j] = lax.fori_loop(
                0, dps - 1, add, g_send[n, j, me].astype(jnp.float32)
            )

    for n in range(2):
        for j in range(slots):
            wait_bytes(w_full.at[n, j, others], w_ssem.at[n, j])
            wait_bytes(g_send.at[n, j, others], g_ssem.at[n, j])

        @pl.when(place < segments - 1)
        def _():
            x_copy(n).wait_send()

        @pl.when(place > 0)
        def _():
            d_copy(n).wait_send()


def train(segments, dps, side, image, cot, taps, rows_live):
    _, slots, rows, width = rows_live.shape
    cells = image.shape[0]
    vmem = pl.BlockSpec(memory_space=pltpu.VMEM)
    dma = pltpu.SemaphoreType.DMA
    bf, f32 = jnp.bfloat16, jnp.float32
    return pl.pallas_call(
        functools.partial(train_kernel, segments, dps, side),
        out_shape=jax.ShapeDtypeStruct((2, slots, rows, width), f32),
        in_specs=[vmem] * 4,
        out_specs=vmem,
        scratch_shapes=[
            pltpu.VMEM((2, slots + 1, cells, width), bf),
            pltpu.VMEM((2, slots + 1, cells, width), bf),
            pltpu.VMEM((2, slots, cells, width), bf),
            pltpu.VMEM((2, slots, cells // SUB, SUB, width), f32),
            pltpu.VMEM((2, slots, dps, rows, width), bf),
            pltpu.VMEM((2, slots, dps, rows, width), bf),
            pltpu.VMEM((2, slots, dps - 1, rows, width), bf),
            pltpu.VMEM((4, cells // SUB, SUB, width), f32),
            pltpu.VMEM((2, slots, 25, SUB, width), f32),
            pltpu.VMEM((width, width), f32),
            dma((2, slots)), dma((2, slots)), dma((2, slots)), dma((2, slots)),
            dma((2,)), dma((2,)), dma((2,)), dma((2,)),
        ],
        compiler_params=pltpu.CompilerParams(
            collective_id=0, has_side_effects=True, vmem_limit_bytes=40 * 1024 * 1024
        ),
        name="train_window",
    )(image, cot, taps, rows_live)


def to_cells(field):
    lead = field.shape[:-3]
    side, width = field.shape[-2], field.shape[-1]
    k = len(lead)
    split = field.reshape(lead + (side // 2, 2, side, width))
    split = jnp.transpose(split, tuple(range(k)) + (k + 1, k + 2, k, k + 3))
    split = jnp.pad(split, ((0, 0),) * (k + 2) + ((0, SUB - side // 2), (0, 0)))
    return split.reshape(lead + (2 * side * SUB, width))


def body(images, cotangent, picks, section_sizes, kernels, weights, first_moment, second_moment):
    segments = lax.axis_size("segment")
    dps = lax.axis_size("dp")
    slots = kernels.shape[0]
    side = images.shape[1]
    total_rows = images.shape[0] * side * side * dps
    taps, w_rows, w_live, m_rows, v_rows = pick(
        picks, section_sizes, kernels, weights, first_moment, second_moment
    )
    summed = train(
        segments, dps, side, to_cells(images[0]), to_cells(cotangent[:, 0]), taps, w_live
    )
    same = (picks[0] == picks[1])[None, :, None, None]
    live = (jnp.arange(slots) < section_sizes[0])[None, :, None, None]
    grad = (summed + jnp.where(same, summed[::-1], 0.0)) / total_rows
    next_m = first_decay * m_rows + (1.0 - first_decay) * grad
    next_v = second_decay * v_rows + (1.0 - second_decay) * grad * grad
    next_w = (
        w_rows.astype(jnp.float32)
        - learn_rate * (next_m / first_bias) / (jnp.sqrt(next_v / second_bias) + adam_epsilon)
    ).astype(jnp.bfloat16)
    return (
        jnp.where(live, next_w, w_rows),
        jnp.where(live, next_m, m_rows),
        jnp.where(live, next_v, v_rows),
    )


def solution(mesh):
    return jax.shard_map(
        body,
        mesh=mesh,
        in_specs=(
            P("dp", None, None, None),
            P(None, "dp", None, None, None),
            P(None, "segment"),
            P("segment"),
            P("segment", None, None, None),
            P("segment", None, "dp", None),
            P("segment", None, "dp", None),
            P("segment", None, "dp", None),
        ),
        out_specs=(
            P(None, "segment", "dp", None),
            P(None, "segment", "dp", None),
            P(None, "segment", "dp", None),
        ),
        check_vma=False,
    )
```

profile of v0, /device:TPU:0, one launch (start us, length us, event | category | flops | bytes accessed | tf_op | source)
XLA Modules:
  0.0 96.9 jit_solution(18251976764394840522)
XLA Ops:
  0.6 0.0 copy-start.3
  0.6 0.0 copy-start.2
  1.4 2.3 %copy.11.k_hbm = bf16[2,48,25,384]{3,2,1,0:T(8,128)(2,1)S(1)} copy(bf16[2,48,25,384]{3,1,2,0:T(8,128)(2,1)} %param.12) | data formatting | bytes 3686400 | tf_op args[4]
  3.7 0.0 copy-done.3
  3.7 0.0 copy-done.2
  3.7 0.0 copy-start
  3.7 3.0 %copy-done = f32[2,48,48,384]{3,2,1,0:T(8,128)S(1)} copy-done((f32[2,48,48,384]{3,2,1,0:T(8,128)S(1)}, f32[2,48,48,384]{3,2,1,0:T(8,128)}, u32[]{:S(2)}) %copy-start) | copy-done | bytes 7077912
  6.7 0.0 copy-start.1
  6.7 3.0 %copy-done.1 = f32[2,48,48,384]{3,2,1,0:T(8,128)S(1)} copy-done((f32[2,48,48,384]{3,2,1,0:T(8,128)S(1)}, f32[2,48,48,384]{3,2,1,0:T(8,128)}, u32[]{:S(2)}) %copy-start.1) | copy-done | bytes 7077912
  9.8 0.0 copy-start.4
  9.8 0.0 copy-start.5
  9.8 1.8 %pick_rows.1 = (bf16[2,2,25,384]{3,2,1,0:T(8,128)(2,1)S(1)}, bf16[2,2,48,384]{3,2,1,0:T(8,128)(2,1)S(1)}, bf16[2,2,48,384]{3,2,1,0:T(8,128)(2,1)S(1)}, f32[2,2,4...) custom-call(s32[2,2]{1,0:T(2,128)S(1)} %copy-done.3, s32[1]{0:T(128)} %copy.18.size_ref, ...), custom_call_target="tpu_custom_call" | custom-call | tf_op jit(solution)/shard_map/pick_rows/pallas_call | solution.py:50
  11.6 0.0 copy-done.4
  11.7 0.1 pad.9
  11.7 0.0 copy-done.5
  11.8 0.1 copy.17
  11.9 83.0 %train_window.1 = f32[2,2,48,384]{3,2,1,0:T(8,128)S(1)} custom-call(bf16[224,384]{1,0:T(8,128)(2,1)S(1)} %bitcast.15, bf16[2,224,384]{2,1,0:T(8,128)(2,1)S(1)} %bitcast.14, bf16[2,2,25,384]{3,2,1,0:T(8,128)(2,1)S(1)} %get-tuple-element.10.k_ref, bf16[2,2,48,384]{3,2,1,0:T(8,128)(2,1)S(1)} %get-tuple-element.11.w_ref), custom_call_target="tpu_custom_call" | custom-call | tf_op jit(solution)/shard_map/train_window/pallas_call | solution.py:368
  94.9 1.0 %fusion = bf16[2,2,48,384]{3,2,1,0:T(8,128)(2,1)} fusion(bf16[2,2,48,384]{3,2,1,0:T(8,128)(2,1)S(1)} %get-tuple-element.8, f32[2,2,48,384]{3,2,1,0:T(8,128)S(1)} %train_window.1, f32[2,2,48,384]{3,2,1,0:T(8,128)S(1)} %get-tuple-element.9, f32[2,2,48,384]{3,2,1,0:T(8,128)S(1)} %get-tuple-element.12, pred[2]{0:T(512)(128)(4,1)S(1)} %compare_bitcast_fusion, ...), kind=kLoop, calls=%fused_computation.5 | loop fusion | flops 1327104 | bytes 1179652 | tf_op jit(solution)/shard_map/jit(_where)/select_n | solution.py:426
  95.9 1.0 %fusion.2 = (f32[2,2,48,384]{3,2,1,0:T(8,128)}, f32[2,2,48,384]{3,2,1,0:T(8,128)}) fusion(f32[2,2,48,384]{3,2,1,0:T(8,128)S(1)} %get-tuple-element.12, f32[2,2,48,384]{3,2,1,0:T(8,128)S(1)} %train_window.1, pred[2]{0:T(512)(128)(4,1)S(1)} %compare_bitcast_fusion, pred[2]{0:T(512)(128)(4,1)S(1)} %iota_compare_fusion, f32[2,2,48,384]{3,2,1,0:T(8,128)S(1)} %get-tuple-element.9), kind=kLoop, calls=%fused_computation.8 | loop fusion | flops 884736 | bytes 1474564 | tf_op jit(solution)/shard_map/jit(_where)/select_n | solution.py:428
  (4 shorter events, 0.1 us)
Async XLA Ops:
  0.6 3.1 %copy-start.3 = (s32[2,2]{1,0:T(2,128)S(1)}, s32[2,2]{1,0:T(2,128)}, u32[]{:S(2)}) copy-start(s32[2,2]{1,0:T(2,128)} %picks_ref.1) | copy-start | bytes 52
  0.6 3.1 %copy-start.2 = (bf16[2,48,48,384]{3,2,1,0:T(8,128)(2,1)S(1)}, bf16[2,48,48,384]{3,2,1,0:T(8,128)(2,1)}, u32[]{:S(2)}) copy-start(bf16[2,48,48,384]{3,2,1,0:T(8,128)(2,1)} %w_hbm.1) | copy-start | bytes 10616836
  3.7 3.0 %copy-start = (f32[2,48,48,384]{3,2,1,0:T(8,128)S(1)}, f32[2,48,48,384]{3,2,1,0:T(8,128)}, u32[]{:S(2)}) copy-start(f32[2,48,48,384]{3,2,1,0:T(8,128)} %m_hbm.1) | copy-start | bytes 21233668
  6.7 3.0 %copy-start.1 = (f32[2,48,48,384]{3,2,1,0:T(8,128)S(1)}, f32[2,48,48,384]{3,2,1,0:T(8,128)}, u32[]{:S(2)}) copy-start(f32[2,48,48,384]{3,2,1,0:T(8,128)} %v_hbm.1) | copy-start | bytes 21233668
  9.8 1.9 %copy-start.4 = (bf16[2,1,14,14,384]{4,0,3,2,1:T(2,128)(2,1)S(1)}, bf16[2,1,14,14,384]{4,0,3,2,1:T(2,128)(2,1)}, u32[]{:S(2)}) copy-start(bf16[2,1,14,14,384]{4,0,3,2,1:T(2,128)(2,1)} %param.9) | copy-start | bytes 903172
  9.8 2.0 %copy-start.5 = (bf16[1,14,14,384]{3,2,1,0:T(8,128)(2,1)S(1)}, bf16[1,14,14,384]{3,2,1,0:T(8,128)(2,1)}, u32[]{:S(2)}) copy-start(bf16[1,14,14,384]{3,2,1,0:T(8,128)(2,1)} %param.8) | copy-start | bytes 451588
where the time goes:
time: 97.1 us; the launch traced here: 96.9 us
  Pallas kernels  84.8 us (87%)
  local copies, waits for them, and re-layouts  8.49 us (9%)
  other arithmetic  2.02 us (2%)
  between operations  1.55 us (2%)
    pallas_call x1, Pallas kernels, train(): pl.pallas_call(functools.partial(train_kernel, segments, dps, side), out_...  83 us
    unnamed x13, local copies, waits for them, and re-layouts  8.29 us

commit v1 on v0

v1 whole, which is shorter than its diff:
```python
import functools

import jax
import jax.numpy as jnp
from jax import lax
from jax.experimental import pallas as pl
from jax.experimental.pallas import tpu as pltpu
from jax.sharding import PartitionSpec as P

first_decay = 0.9
second_decay = 0.999
learn_rate = 0.01
adam_epsilon = 1e-08
first_bias = 1.0 - 0.9**10
second_bias = 1.0 - 0.999**10
MESH = pl.DeviceIdType.MESH
SUB = 8
LANES = 128


def pick_kernel(
    picks_ref, size_ref, k_hbm, w_hbm, m_hbm, v_hbm, k_out, w_out, live_out, m_out, v_out, sem
):
    slots = w_out.shape[1]
    copies = []
    for n in range(2):
        for j in range(slots):
            o = picks_ref[n, j]
            for i, (src, dst) in enumerate(
                ((w_hbm, w_out), (k_hbm, k_out), (m_hbm, m_out), (v_hbm, v_out))
            ):
                copy = pltpu.make_async_copy(src.at[j, o], dst.at[n, j], sem.at[i, n, j])
                copy.start()
                copies.append(copy)
    for copy in copies:
        copy.wait()
    for j in range(slots):
        scale = jnp.where(j < size_ref[0], 1.0, 0.0).astype(jnp.float32)
        for n in range(2):
            live_out[n, j] = (w_out[n, j].astype(jnp.float32) * scale).astype(jnp.bfloat16)


def pick(picks, sizes, kernels, weights, first, second):
    slots, _, taps, width = kernels.shape
    rows = weights.shape[2]
    shape = jax.ShapeDtypeStruct
    vmem = pl.BlockSpec(memory_space=pltpu.VMEM)
    smem = pl.BlockSpec(memory_space=pltpu.SMEM)
    hbm = pl.BlockSpec(memory_space=pl.ANY)
    return pl.pallas_call(
        pick_kernel,
        out_shape=(
            shape((2, slots, taps, width), jnp.bfloat16),
            shape((2, slots, rows, width), jnp.bfloat16),
            shape((2, slots, rows, width), jnp.bfloat16),
            shape((2, slots, rows, width), jnp.float32),
            shape((2, slots, rows, width), jnp.float32),
        ),
        in_specs=[smem, smem, hbm, hbm, hbm, hbm],
        out_specs=(vmem,) * 5,
        scratch_shapes=[pltpu.SemaphoreType.DMA((4, 2, slots))],
        compiler_params=pltpu.CompilerParams(vmem_limit_bytes=56 * 1024 * 1024),
        name="pick_rows",
    )(picks, sizes, kernels, weights, first, second)


def put_shifts(shifted, value, lanes):
    shifted[1, :, :, lanes] = value
    shifted[0, :, :, lanes] = pltpu.roll(value, 1, 1)
    shifted[2, :, :, lanes] = pltpu.roll(value, SUB - 1, 1)


def conv_columns(shifted, taps, side, lanes, emit):
    weights = [taps(t) for t in range(25)]
    loaded = {}

    def cell(sh, r, q):
        if (sh, r, q) not in loaded:
            loaded[sh, r, q] = shifted[sh + 1, r * side + q, :, lanes]
        return loaded[sh, r, q]

    for q in range(side):
        for r in range(2):
            parts = []
            for e in range(-2, 3):
                if not 0 <= q + e < side:
                    continue
                part = None
                for a in range(-2, 3):
                    sh, rr = (r + a) // 2, (r + a) % 2
                    term = weights[(a + 2) * 5 + e + 2] * cell(sh, rr, q + e)
                    part = term if part is None else part + term
                parts.append(part)
            total = parts[0]
            for part in parts[1:]:
                total = total + part
            emit(r, q, total)


def train_kernel(
    segments, dps, side,
    image_ref, cot_ref, k_ref, w_ref,
    g_out,
    x_buf, up_buf, h_buf, act_buf, k_full, w_full, g_send, g_recv, shifted, taps_wide,
    joined, k_ssem, k_rsem, w_ssem, w_rsem, g_ssem, g_rsem,
):
    place = lax.axis_index("segment")
    me = lax.axis_index("dp")
    slots = w_ref.shape[1]
    rows = w_ref.shape[2]
    width = w_ref.shape[3]
    blocks = slots * segments
    cells = x_buf.shape[1]
    tiles = width // LANES
    aligned = rows % 16 == 0
    share = segments // 2
    net = place // share
    works = lax.rem(place, share) == 0
    idle = lax.rem(place, share) != 0

    barrier = pltpu.get_barrier_semaphore()

    def greet(target, d):
        @pl.when(jnp.logical_or(target != place, d != me))
        def _():
            pl.semaphore_signal(
                barrier, inc=1, device_id={"segment": target, "dp": d}, device_id_type=MESH
            )

    def greet_workers(d, carry):
        for n in range(2):
            greet(n * share, d)
        return carry

    lax.fori_loop(0, dps, greet_workers, 0)

    @pl.when(works)
    def _():
        def greet_rest(d, carry):
            for n in range(2):
                for k in range(1, share):
                    greet(n * share + k, d)
            return carry

        lax.fori_loop(0, dps, greet_rest, 0)
        pl.semaphore_wait(barrier, segments * dps - 1)

    @pl.when(idle)
    def _():
        pl.semaphore_wait(barrier, 2 * dps)

    def send(src, dst, send_sem, recv_sem, target, d):
        here = jnp.logical_and(target == place, d == me)

        @pl.when(here)
        def _():
            pltpu.make_async_copy(src, dst, recv_sem).start()

        @pl.when(jnp.logical_not(here))
        def _():
            pltpu.make_async_remote_copy(
                src_ref=src,
                dst_ref=dst,
                send_sem=send_sem,
                recv_sem=recv_sem,
                device_id={"segment": target, "dp": d},
                device_id_type=MESH,
            ).start()

    def wait_bytes(ref, sem):
        pltpu.make_async_copy(ref, ref, sem).wait()

    for n in range(2):
        send(k_ref.at[n], k_full.at[place], k_ssem.at[n], k_rsem.at[place], n * share, me)
    for j in range(slots):

        def send_rows(i, carry):
            d = lax.rem(me + i, dps)
            for n in range(2):
                send(
                    w_ref.at[n, j],
                    w_full.at[place * slots + j, me],
                    w_ssem.at[n, j],
                    w_rsem.at[place * slots + j],
                    n * share,
                    d,
                )
            return carry

        lax.fori_loop(0, dps, send_rows, 0)

    inside = lax.broadcasted_iota(jnp.int32, (SUB, LANES), 0) < side // 2

    def lane_slice(ct):
        return pl.ds(pl.multiple_of(ct * LANES, LANES), LANES)

    def weight_of(b):
        if aligned:
            return w_full[b].reshape(width, width)
        for k in range(dps):
            joined[k * rows : (k + 1) * rows] = w_full[b, k].astype(jnp.float32)
        return joined[...].astype(jnp.bfloat16)

    def store_grad(b, grad):
        if aligned:
            g_send[b] = grad.astype(jnp.bfloat16).reshape(dps, rows, width)
        else:
            joined[...] = grad
            for k in range(dps):
                g_send[b, k] = joined[k * rows : (k + 1) * rows].astype(jnp.bfloat16)

    def widen(s, carry):
        wait_bytes(k_full.at[s], k_rsem.at[s])
        for j in range(slots):
            for t in range(25):
                taps_wide[s * slots + j, t] = jnp.broadcast_to(
                    k_full[s, j, t : t + 1, :].astype(jnp.float32), (SUB, width)
                )
        return carry

    def forward(b, carry):
        def tile(ct, carry):
            lanes = lane_slice(ct)
            value = x_buf[b, :, lanes].astype(jnp.float32).reshape(2 * side, SUB, LANES)
            put_shifts(shifted, value, lanes)

            def emit(r, q, u):
                s = 0.5 * jnp.tanh(0.5 * u) + 0.5
                at = r * side + q
                act_buf[b, at, :, lanes] = jnp.where(inside, s * (1.0 + u * (1.0 - s)), 0.0)
                shifted[3, at, :, lanes] = jnp.where(inside, u * s, 0.0)

            conv_columns(shifted, lambda t: taps_wide[b, t, :, lanes], side, lanes, emit)
            h_buf[b, :, lanes] = (
                shifted[3, :, :, lanes].reshape(cells, LANES).astype(jnp.bfloat16)
            )
            return carry

        lax.fori_loop(0, tiles, tile, 0)
        wait_bytes(w_full.at[b], w_rsem.at[b])

        @pl.when(b < blocks - 1)
        def _():
            update = jnp.dot(h_buf[b], weight_of(b), preferred_element_type=jnp.float32)
            x_buf[b + 1] = (x_buf[b].astype(jnp.float32) + update).astype(jnp.bfloat16)

        return carry

    def backward(i, carry):
        b = blocks - 1 - i
        grad = lax.dot_general(
            h_buf[b],
            up_buf[b + 1],
            (((0,), (0,)), ((), ())),
            preferred_element_type=jnp.float32,
        )
        store_grad(b, grad)

        def send_grad(k, carry):
            owner = lax.rem(me + k, dps)
            send(
                g_send.at[b, owner],
                g_recv.at[net, lax.rem(b, slots), me],
                g_ssem.at[b],
                g_rsem.at[net, lax.rem(b, slots)],
                b // slots,
                owner,
            )
            return carry

        lax.fori_loop(0, dps, send_grad, 0)

        @pl.when(b > 0)
        def _():
            back = lax.dot_general(
                up_buf[b + 1],
                weight_of(b),
                (((1,), (1,)), ((), ())),
                preferred_element_type=jnp.float32,
            )
            shifted[3] = back.reshape(2 * side, SUB, width)

            def tile(ct, carry):
                lanes = lane_slice(ct)
                put_shifts(shifted, shifted[3, :, :, lanes] * act_buf[b, :, :, lanes], lanes)

                def emit(r, q, total):
                    shifted[3, r * side + q, :, lanes] = jnp.where(inside, total, 0.0)

                conv_columns(
                    shifted, lambda t: taps_wide[b, 24 - t, :, lanes], side, lanes, emit
                )
                up_buf[b, :, lanes] = (
                    up_buf[b + 1, :, lanes].astype(jnp.float32)
                    + shifted[3, :, :, lanes].reshape(cells, LANES)
                ).astype(jnp.bfloat16)
                return carry

            lax.fori_loop(0, tiles, tile, 0)

        return carry

    @pl.when(works)
    def _():
        x_buf[0] = image_ref[...]
        up_buf[blocks] = cot_ref[net]
        lax.fori_loop(0, segments, widen, 0)
        lax.fori_loop(0, blocks, forward, 0)
        lax.fori_loop(0, blocks, backward, 0)

    for j in reversed(range(slots)):
        for n in range(2):
            wait_bytes(g_recv.at[n, j], g_rsem.at[n, j])

            def add(d, total):
                return total + g_recv[n, j, d].astype(jnp.float32)

            g_out[n, j] = lax.fori_loop(0, dps, add, jnp.zeros((rows, width), jnp.float32))

    most = pl.ds(0, dps - 1)
    for n in range(2):
        mine = place == n * share

        @pl.when(jnp.logical_not(mine))
        def _():
            wait_bytes(k_ref.at[n], k_ssem.at[n])
            for j in range(slots):
                wait_bytes(g_recv.at[n, j], w_ssem.at[n, j])

        @pl.when(mine)
        def _():
            for j in range(slots):
                wait_bytes(g_recv.at[n, j, most], w_ssem.at[n, j])

    @pl.when(works)
    def _():
        def drain(b, carry):
            own = b // slots == place

            @pl.when(own)
            def _():
                wait_bytes(g_send.at[b, most], g_ssem.at[b])

            @pl.when(jnp.logical_not(own))
            def _():
                wait_bytes(g_send.at[b], g_ssem.at[b])

            return carry

        lax.fori_loop(0, blocks, drain, 0)


def train(segments, dps, side, image, cot, taps, rows_live):
    _, slots, rows, width = rows_live.shape
    cells = image.shape[0]
    blocks = slots * segments
    vmem = pl.BlockSpec(memory_space=pltpu.VMEM)
    dma = pltpu.SemaphoreType.DMA
    bf, f32 = jnp.bfloat16, jnp.float32
    return pl.pallas_call(
        functools.partial(train_kernel, segments, dps, side),
        out_shape=jax.ShapeDtypeStruct((2, slots, rows, width), f32),
        in_specs=[vmem] * 4,
        out_specs=vmem,
        scratch_shapes=[
            pltpu.VMEM((blocks, cells, width), bf),
            pltpu.VMEM((blocks + 1, cells, width), bf),
            pltpu.VMEM((blocks, cells, width), bf),
            pltpu.VMEM((blocks, cells // SUB, SUB, width), f32),
            pltpu.VMEM((segments, slots, taps.shape[2], width), bf),
            pltpu.VMEM((blocks, dps, rows, width), bf),
            pltpu.VMEM((blocks, dps, rows, width), bf),
            pltpu.VMEM((2, slots, dps, rows, width), bf),
            pltpu.VMEM((4, cells // SUB, SUB, width), f32),
            pltpu.VMEM((blocks, 25, SUB, width), f32),
            pltpu.VMEM((width, width), f32),
            dma((2,)), dma((segments,)),
            dma((2, slots)), dma((blocks,)), dma((blocks,)), dma((2, slots)),
        ],
        compiler_params=pltpu.CompilerParams(
            collective_id=0, has_side_effects=True, vmem_limit_bytes=52 * 1024 * 1024
        ),
        name="train_window",
    )(image, cot, taps, rows_live)


def to_cells(field):
    lead = field.shape[:-3]
    side, width = field.shape[-2], field.shape[-1]
    k = len(lead)
    split = field.reshape(lead + (side // 2, 2, side, width))
    split = jnp.transpose(split, tuple(range(k)) + (k + 1, k + 2, k, k + 3))
    split = jnp.pad(split, ((0, 0),) * (k + 2) + ((0, SUB - side // 2), (0, 0)))
    return split.reshape(lead + (2 * side * SUB, width))


def body(images, cotangent, picks, section_sizes, kernels, weights, first_moment, second_moment):
    segments = lax.axis_size("segment")
    dps = lax.axis_size("dp")
    slots = kernels.shape[0]
    side = images.shape[1]
    total_rows = images.shape[0] * side * side * dps
    taps, w_rows, w_live, m_rows, v_rows = pick(
        picks, section_sizes, kernels, weights, first_moment, second_moment
    )
    summed = train(
        segments, dps, side, to_cells(images[0]), to_cells(cotangent[:, 0]), taps, w_live
    )
    same = (picks[0] == picks[1])[None, :, None, None]
    live = (jnp.arange(slots) < section_sizes[0])[None, :, None, None]
    grad = (summed + jnp.where(same, summed[::-1], 0.0)) / total_rows
    next_m = first_decay * m_rows + (1.0 - first_decay) * grad
    next_v = second_decay * v_rows + (1.0 - second_decay) * grad * grad
    next_w = (
        w_rows.astype(jnp.float32)
        - learn_rate * (next_m / first_bias) / (jnp.sqrt(next_v / second_bias) + adam_epsilon)
    ).astype(jnp.bfloat16)
    return (
        jnp.where(live, next_w, w_rows),
        jnp.where(live, next_m, m_rows),
        jnp.where(live, next_v, v_rows),
    )


def solution(mesh):
    return jax.shard_map(
        body,
        mesh=mesh,
        in_specs=(
            P("dp", None, None, None),
            P(None, "dp", None, None, None),
            P(None, "segment"),
            P("segment"),
            P("segment", None, None, None),
            P("segment", None, "dp", None),
            P("segment", None, "dp", None),
            P("segment", None, "dp", None),
        ),
        out_specs=(
            P(None, "segment", "dp", None),
            P(None, "segment", "dp", None),
            P(None, "segment", "dp", None),
        ),
        check_vma=False,
    )
```

time: 97.1 us -> 80.7 us (0.83)
  Pallas kernels: 84.8 us -> 70.4 us
  local copies, waits for them, and re-layouts: 8.49 us -> 5.43 us
  other arithmetic: 2.02 us -> 3.23 us
    pallas_call x1, Pallas kernels: 83 us -> 67.3 us  [train(): pl.pallas_call(functools.partial(train_kernel, segments, dps, side), out_...]
    unnamed x13 -> x15, local copies, waits for them, and re-layouts: 8.29 us -> 5.22 us
    pallas_call x1, Pallas kernels: 1.85 us -> 3.13 us  [pick(): pl.pallas_call(pick_kernel, out_shape=(shape((2, slots, taps, width), jnp...]
    select_n x1, other arithmetic: 0.99 us -> 2.21 us  [body(): jnp.where(live, next_w, w_rows)]
where the time goes in v1:
time: 80.7 us; the launch traced here: 80.4 us
  Pallas kernels  70.4 us (87%)
  local copies, waits for them, and re-layouts  5.43 us (7%)
  other arithmetic  3.23 us (4%)
  between operations  1.39 us (2%)
    pallas_call x1, Pallas kernels, train(): pl.pallas_call(functools.partial(train_kernel, segments, dps, side), out_...  67.3 us
    unnamed x15, local copies, waits for them, and re-layouts  5.22 us
    pallas_call x1, Pallas kernels, pick(): pl.pallas_call(pick_kernel, out_shape=(shape((2, slots, taps, width), jnp...  3.13 us
    select_n x1, other arithmetic, body(): jnp.where(live, next_w, w_rows)  2.21 us

profile of v1, /device:TPU:0, one launch (start us, length us, event | category | flops | bytes accessed | tf_op | source)
XLA Modules:
  0.0 80.4 jit_solution(9998984848003554019)
XLA Ops:
  1.3 3.4 %copy.11.k_hbm = bf16[2,48,25,384]{3,2,1,0:T(8,128)(2,1)} copy(bf16[2,48,25,384]{3,1,2,0:T(8,128)(2,1)} %param.12) | data formatting | bytes 3686400 | tf_op args[4]
  4.7 0.0 copy-start.4
  4.7 0.0 copy-start.5
  4.7 0.0 copy-start.6
  4.7 3.1 %pick_rows.1 = (bf16[2,2,25,384]{3,2,1,0:T(8,128)(2,1)}, bf16[2,2,48,384]{3,2,1,0:T(8,128)(2,1)}, bf16[2,2,48,384]{3,2,1,0:T(8,128)(2,1)}, f32[2,2,48,384]{3,2,1,0:T(8,128)}, f32[2,2,48,384]{3,2,1,0:T(8,128)}) custom-call(s32[2,2]{1,0:T(2,128)} %picks_ref.1, s32[1]{0:T(128)} %copy.18.size_ref, bf16[2,48,25,384]{3,2,1,0:T(8,128)(2,1)} %copy.11.k_hbm, ...), custom_call_target="tpu_custom_call" | custom-call | tf_op jit(solution)/shard_map/pick_rows/pallas_call | solution.py:50
  7.8 0.0 copy-start.2
  7.8 0.0 copy-start.3
  7.8 0.0 copy-done.4
  7.9 0.1 pad.9
  8.0 0.0 copy-done.5
  8.0 0.1 copy.17
  8.1 0.0 copy-start
  8.1 0.9 %copy-done = bf16[2,2,48,384]{3,2,1,0:T(8,128)(2,1)S(1)} copy-done((bf16[2,2,48,384]{3,2,1,0:T(8,128)(2,1)S(1)}, bf16[2,2,48,384]{3,2,1,0:T(8,128)(2,1)}, u32[]{:S(2)}) %copy-start) | copy-done | bytes 147480
  9.0 0.0 copy-start.1
  9.0 0.9 %copy-done.1 = bf16[2,2,25,384]{3,2,1,0:T(8,128)(2,1)S(1)} copy-done((bf16[2,2,25,384]{3,2,1,0:T(8,128)(2,1)S(1)}, bf16[2,2,25,384]{3,2,1,0:T(8,128)(2,1)}, u32[]{:S(2)}) %copy-start.1) | copy-done | bytes 76824
  9.9 67.3 %train_window.1 = f32[2,2,48,384]{3,2,1,0:T(8,128)S(1)} custom-call(bf16[224,384]{1,0:T(8,128)(2,1)S(1)} %bitcast.15, bf16[2,224,384]{2,1,0:T(8,128)(2,1)S(1)} %bitcast.14, bf16[2,2,25,384]{3,2,1,0:T(8,128)(2,1)S(1)} %copy-done.1, bf16[2,2,48,384]{3,2,1,0:T(8,128)(2,1)S(1)} %copy-done), custom_call_target="tpu_custom_call" | custom-call | tf_op jit(solution)/shard_map/train_window/pallas_call | solution.py:360
  77.2 0.0 copy-done.6
  77.2 2.2 %fusion = bf16[2,2,48,384]{3,2,1,0:T(8,128)(2,1)} fusion(bf16[2,2,48,384]{3,2,1,0:T(8,128)(2,1)} %get-tuple-element.8, f32[2,2,48,384]{3,2,1,0:T(8,128)S(1)} %train_window.1, f32[2,2,48,384]{3,2,1,0:T(8,128)} %get-tuple-element.9, f32[2,2,48,384]{3,2,1,0:T(8,128)} %get-tuple-element.12, pred[2]{0:T(512)(128)(4,1)S(1)} %compare_bitcast_fusion, ...), kind=kLoop, calls=%fused_computation.5 | loop fusion | flops 1327104 | bytes 1179652 | tf_op jit(solution)/shard_map/jit(_where)/select_n | solution.py:419
  79.4 0.0 copy-done.2
  79.4 0.0 copy-done.3
  79.4 1.0 %fusion.2 = (f32[2,2,48,384]{3,2,1,0:T(8,128)}, f32[2,2,48,384]{3,2,1,0:T(8,128)}) fusion(f32[2,2,48,384]{3,2,1,0:T(8,128)S(1)} %copy-done.3, f32[2,2,48,384]{3,2,1,0:T(8,128)S(1)} %train_window.1, pred[2]{0:T(512)(128)(4,1)S(1)} %compare_bitcast_fusion, pred[2]{0:T(512)(128)(4,1)S(1)} %iota_compare_fusion, f32[2,2,48,384]{3,2,1,0:T(8,128)S(1)} %copy-done.2), kind=kLoop, calls=%fused_computation.8 | loop fusion | flops 884736 | bytes 1474564 | tf_op jit(solution)/shard_map/jit(_where)/select_n | solution.py:421
  (4 shorter events, 0.1 us)
Async XLA Ops:
  4.7 3.2 %copy-start.4 = (bf16[2,1,14,14,384]{4,0,3,2,1:T(2,128)(2,1)S(1)}, bf16[2,1,14,14,384]{4,0,3,2,1:T(2,128)(2,1)}, u32[]{:S(2)}) copy-start(bf16[2,1,14,14,384]{4,0,3,2,1:T(2,128)(2,1)} %param.9) | copy-start | bytes 903172
  4.7 3.3 %copy-start.5 = (bf16[1,14,14,384]{3,2,1,0:T(8,128)(2,1)S(1)}, bf16[1,14,14,384]{3,2,1,0:T(8,128)(2,1)}, u32[]{:S(2)}) copy-start(bf16[1,14,14,384]{3,2,1,0:T(8,128)(2,1)} %param.8) | copy-start | bytes 451588
  4.7 72.5 %copy-start.6 = (s32[2,2]{1,0:T(2,128)S(1)}, s32[2,2]{1,0:T(2,128)}, u32[]{:S(2)}) copy-start(s32[2,2]{1,0:T(2,128)} %picks_ref.1) | copy-start | bytes 52
  7.8 71.6 %copy-start.2 = (f32[2,2,48,384]{3,2,1,0:T(8,128)S(1)}, f32[2,2,48,384]{3,2,1,0:T(8,128)}, u32[]{:S(2)}) copy-start(f32[2,2,48,384]{3,2,1,0:T(8,128)} %get-tuple-element.9) | copy-start | bytes 884740
  7.8 71.6 %copy-start.3 = (f32[2,2,48,384]{3,2,1,0:T(8,128)S(1)}, f32[2,2,48,384]{3,2,1,0:T(8,128)}, u32[]{:S(2)}) copy-start(f32[2,2,48,384]{3,2,1,0:T(8,128)} %get-tuple-element.12) | copy-start | bytes 884740
  8.1 0.9 %copy-start = (bf16[2,2,48,384]{3,2,1,0:T(8,128)(2,1)S(1)}, bf16[2,2,48,384]{3,2,1,0:T(8,128)(2,1)}, u32[]{:S(2)}) copy-start(bf16[2,2,48,384]{3,2,1,0:T(8,128)(2,1)} %get-tuple-element.11.w_ref) | copy-start | bytes 442372
  9.0 0.9 %copy-start.1 = (bf16[2,2,25,384]{3,2,1,0:T(8,128)(2,1)S(1)}, bf16[2,2,25,384]{3,2,1,0:T(8,128)(2,1)}, u32[]{:S(2)}) copy-start(bf16[2,2,25,384]{3,2,1,0:T(8,128)(2,1)} %get-tuple-element.10.k_ref) | copy-start | bytes 230404

commit v2 on v1

--- a/solution.py
+++ b/solution.py
@@ -18,29 +18,40 @@
 LANES = 128
 
 
-def pick_kernel(
-    picks_ref, size_ref, k_hbm, w_hbm, m_hbm, v_hbm, k_out, w_out, live_out, m_out, v_out, sem
-):
-    slots = w_out.shape[1]
+GROUP = 16
+
+
+def pick_kernel(picks_ref, size_ref, k_hbm, w_hbm, k_out, live_out, k_buf, sem):
+    slots = live_out.shape[1]
     copies = []
     for n in range(2):
         for j in range(slots):
             o = picks_ref[n, j]
-            for i, (src, dst) in enumerate(
-                ((w_hbm, w_out), (k_hbm, k_out), (m_hbm, m_out), (v_hbm, v_out))
-            ):
-                copy = pltpu.make_async_copy(src.at[j, o], dst.at[n, j], sem.at[i, n, j])
-                copy.start()
-                copies.append(copy)
-    for copy in copies:
-        copy.wait()
-    for j in range(slots):
-        scale = jnp.where(j < size_ref[0], 1.0, 0.0).astype(jnp.float32)
-        for n in range(2):
-            live_out[n, j] = (w_out[n, j].astype(jnp.float32) * scale).astype(jnp.bfloat16)
-
-
-def pick(picks, sizes, kernels, weights, first, second):
+            start = pl.multiple_of((o // GROUP) * GROUP, GROUP)
+            copies.append(
+                (
+                    pltpu.make_async_copy(w_hbm.at[j, o], live_out.at[n, j], sem.at[0, n, j]),
+                    pltpu.make_async_copy(
+                        k_hbm.at[j, :, pl.ds(start, GROUP)], k_buf.at[n, j], sem.at[1, n, j]
+                    ),
+                )
+            )
+    for pair in copies:
+        for copy in pair:
+            copy.start()
+    for n in range(2):
+        for j in range(slots):
+            for copy in copies[n * slots + j]:
+                copy.wait()
+            scale = jnp.where(j < size_ref[0], 1.0, 0.0).astype(jnp.float32)
+            live_out[n, j] = (live_out[n, j].astype(jnp.float32) * scale).astype(jnp.bfloat16)
+            block = k_buf[n, j].astype(jnp.float32)
+            row = lax.broadcasted_iota(jnp.int32, block.shape, 1)
+            wanted = row == picks_ref[n, j] % GROUP
+            k_out[n, j] = jnp.sum(jnp.where(wanted, block, 0.0), axis=1).astype(jnp.bfloat16)
+
+
+def pick(picks, sizes, kernels, weights):
     slots, _, taps, width = kernels.shape
     rows = weights.shape[2]
     shape = jax.ShapeDtypeStruct
@@ -52,16 +63,67 @@
         out_shape=(
             shape((2, slots, taps, width), jnp.bfloat16),
             shape((2, slots, rows, width), jnp.bfloat16),
-            shape((2, slots, rows, width), jnp.bfloat16),
-            shape((2, slots, rows, width), jnp.float32),
-            shape((2, slots, rows, width), jnp.float32),
         ),
-        in_specs=[smem, smem, hbm, hbm, hbm, hbm],
-        out_specs=(vmem,) * 5,
-        scratch_shapes=[pltpu.SemaphoreType.DMA((4, 2, slots))],
+        in_specs=[smem, smem, hbm, hbm],
+        out_specs=(vmem,) * 2,
+        scratch_shapes=[
+            pltpu.VMEM((2, slots, taps, GROUP, width), jnp.bfloat16),
+            pltpu.SemaphoreType.DMA((2, 2, slots)),
+        ],
         compiler_params=pltpu.CompilerParams(vmem_limit_bytes=56 * 1024 * 1024),
         name="pick_rows",
-    )(picks, sizes, kernels, weights, first, second)
+    )(picks, sizes, jnp.transpose(kernels, (0, 2, 1, 3)), weights)
+
+
+def adam_kernel(
+    total_rows, picks_ref, size_ref, g_ref, w_hbm, m_hbm, v_hbm,
+    w_out, m_out, v_out, w_buf, m_buf, v_buf, sem,
+):
+    slots = w_out.shape[1]
+    copies = []
+    for n in range(2):
+        for j in range(slots):
+            o = picks_ref[n, j]
+            for i, (src, dst) in enumerate(((w_hbm, w_buf), (m_hbm, m_buf), (v_hbm, v_buf))):
+                copy = pltpu.make_async_copy(src.at[j, o], dst.at[n, j], sem.at[i, n, j])
+                copy.start()
+                copies.append(copy)
+    for n in range(2):
+        for j in range(slots):
+            for copy in copies[:3]:
+                copy.wait()
+            copies = copies[3:]
+            other = g_ref[1 - n, j]
+            same = picks_ref[0, j] == picks_ref[1, j]
+            grad = (g_ref[n, j] + jnp.where(same, other, jnp.zeros_like(other))) / total_rows
+            weight, m_row, v_row = w_buf[n, j], m_buf[n, j], v_buf[n, j]
+            next_m = first_decay * m_row + (1.0 - first_decay) * grad
+            next_v = second_decay * v_row + (1.0 - second_decay) * grad * grad
+            next_w = weight.astype(jnp.float32) - learn_rate * (next_m / first_bias) / (
+                jnp.sqrt(next_v / second_bias) + adam_epsilon
+            )
+            live = j < size_ref[0]
+            w_out[n, j] = jnp.where(live, next_w, weight.astype(jnp.float32)).astype(jnp.bfloat16)
+            m_out[n, j] = jnp.where(live, next_m, m_row)
+            v_out[n, j] = jnp.where(live, next_v, v_row)
+
+
+def adam(total_rows, picks, sizes, summed, weights, first, second):
+    shape = summed.shape
+    vmem = pl.BlockSpec(memory_space=pltpu.VMEM)
+    smem = pl.BlockSpec(memory_space=pltpu.SMEM)
+    hbm = pl.BlockSpec(memory_space=pl.ANY)
+    types = (jnp.bfloat16, jnp.float32, jnp.float32)
+    return pl.pallas_call(
+        functools.partial(adam_kernel, total_rows),
+        out_shape=tuple(jax.ShapeDtypeStruct(shape, t) for t in types),
+        in_specs=[smem, smem, vmem, hbm, hbm, hbm],
+        out_specs=(vmem,) * 3,
+        scratch_shapes=[pltpu.VMEM(shape, t) for t in types]
+        + [pltpu.SemaphoreType.DMA((3,) + shape[:2])],
+        compiler_params=pltpu.CompilerParams(vmem_limit_bytes=56 * 1024 * 1024),
+        name="adam_rows",
+    )(picks, sizes, summed, weights, first, second)
 
 
 def put_shifts(shifted, value, lanes):
@@ -102,7 +164,8 @@
     image_ref, cot_ref, k_ref, w_ref,
     g_out,
     x_buf, up_buf, h_buf, act_buf, k_full, w_full, g_send, g_recv, shifted, taps_wide,
-    joined, k_ssem, k_rsem, w_ssem, w_rsem, g_ssem, g_rsem,
+    stage, h_in, up_in, joined,
+    k_ssem, k_rsem, w_ssem, s_rsem, f_ssem, w_rsem, h_ssem, h_rsem, u_ssem, u_rsem, g_ssem, g_rsem,
 ):
     place = lax.axis_index("segment")
     me = lax.axis_index("dp")
@@ -116,38 +179,31 @@
     share = segments // 2
     net = place // share
     works = lax.rem(place, share) == 0
-    idle = lax.rem(place, share) != 0
+    helps = lax.rem(place, share) == 1
+    half = dps // 2
+    low = lax.rem(me, 2)
 
     barrier = pltpu.get_barrier_semaphore()
 
-    def greet(target, d):
-        @pl.when(jnp.logical_or(target != place, d != me))
-        def _():
-            pl.semaphore_signal(
-                barrier, inc=1, device_id={"segment": target, "dp": d}, device_id_type=MESH
-            )
-
-    def greet_workers(d, carry):
-        for n in range(2):
-            greet(n * share, d)
+    def greet(d, carry):
+        for target in range(segments):
+
+            @pl.when(jnp.logical_or(target != place, d != me))
+            def _():
+                pl.semaphore_signal(
+                    barrier, inc=1, device_id={"segment": target, "dp": d}, device_id_type=MESH
+                )
+
         return carry
 
-    lax.fori_loop(0, dps, greet_workers, 0)
+    lax.fori_loop(0, dps, greet, 0)
 
     @pl.when(works)
     def _():
-        def greet_rest(d, carry):
-            for n in range(2):
-                for k in range(1, share):
-                    greet(n * share + k, d)
-            return carry
-
-        lax.fori_loop(0, dps, greet_rest, 0)
-        pl.semaphore_wait(barrier, segments * dps - 1)
-
-    @pl.when(idle)
-    def _():
-        pl.semaphore_wait(barrier, 2 * dps)
+        x_buf[0] = image_ref[...]
+        up_buf[blocks] = cot_ref[net]
+
+    pl.semaphore_wait(barrier, segments * dps - 1)
 
     def send(src, dst, send_sem, recv_sem, target, d):
         here = jnp.logical_and(target == place, d == me)
@@ -175,19 +231,19 @@
     for j in range(slots):
 
         def send_rows(i, carry):
-            d = lax.rem(me + i, dps)
+            hi = lax.rem(me // 2 + i, half)
             for n in range(2):
                 send(
                     w_ref.at[n, j],
-                    w_full.at[place * slots + j, me],
+                    stage.at[place * slots + j, me // 2],
                     w_ssem.at[n, j],
-                    w_rsem.at[place * slots + j],
-                    n * share,
-                    d,
+                    s_rsem.at[place * slots + j],
+                    n * share + 1,
+                    hi * 2 + low,
                 )
             return carry
 
-        lax.fori_loop(0, dps, send_rows, 0)
+        lax.fori_loop(0, half, send_rows, 0)
 
     inside = lax.broadcasted_iota(jnp.int32, (SUB, LANES), 0) < side // 2
 
@@ -198,7 +254,7 @@
         if aligned:
             return w_full[b].reshape(width, width)
         for k in range(dps):
-            joined[k * rows : (k + 1) * rows] = w_full[b, k].astype(jnp.float32)
+            joined[k * rows : (k + 1) * rows] = w_full[b, k // 2, k % 2].astype(jnp.float32)
         return joined[...].astype(jnp.bfloat16)
 
     def store_grad(b, grad):
@@ -208,6 +264,35 @@
             joined[...] = grad
             for k in range(dps):
                 g_send[b, k] = joined[k * rows : (k + 1) * rows].astype(jnp.bfloat16)
+
+    def forward_rows(b, carry):
+        wait_bytes(stage.at[b], s_rsem.at[b])
+        for k in range(2):
+            pltpu.make_async_remote_copy(
+                src_ref=stage.at[b],
+                dst_ref=w_full.at[b, :, low],
+                send_sem=f_ssem.at[b],
+                recv_sem=w_rsem.at[b],
+                device_id={"segment": place - 1, "dp": (me // 2) * 2 + lax.rem(low + k, 2)},
+                device_id_type=MESH,
+            ).start()
+        return carry
+
+    def hand(src, dst, send_sem, recv_sem):
+        return pltpu.make_async_remote_copy(
+            src_ref=src,
+            dst_ref=dst,
+            send_sem=send_sem,
+            recv_sem=recv_sem,
+            device_id={"segment": lax.rem(place + 1, segments)},
+            device_id_type=MESH,
+        )
+
+    def hand_h(b):
+        return hand(h_buf.at[b], h_in.at[b], h_ssem.at[b], h_rsem.at[b])
+
+    def hand_up(b):
+        return hand(up_buf.at[b + 1], up_in.at[b], u_ssem.at[b], u_rsem.at[b])
 
     def widen(s, carry):
         wait_bytes(k_full.at[s], k_rsem.at[s])
@@ -237,6 +322,7 @@
             return carry
 
         lax.fori_loop(0, tiles, tile, 0)
+        hand_h(b).start()
         wait_bytes(w_full.at[b], w_rsem.at[b])
 
         @pl.when(b < blocks - 1)
@@ -246,11 +332,13 @@
 
         return carry
 
-    def backward(i, carry):
+    def gradient(i, carry):
         b = blocks - 1 - i
+        hand_h(b).wait_recv()
+        hand_up(b).wait_recv()
         grad = lax.dot_general(
-            h_buf[b],
-            up_buf[b + 1],
+            h_in[b],
+            up_in[b],
             (((0,), (0,)), ((), ())),
             preferred_element_type=jnp.float32,
         )
@@ -269,6 +357,11 @@
             return carry
 
         lax.fori_loop(0, dps, send_grad, 0)
+        return carry
+
+    def backward(i, carry):
+        b = blocks - 1 - i
+        hand_up(b).start()
 
         @pl.when(b > 0)
         def _():
@@ -302,12 +395,15 @@
 
     @pl.when(works)
     def _():
-        x_buf[0] = image_ref[...]
-        up_buf[blocks] = cot_ref[net]
         lax.fori_loop(0, segments, widen, 0)
         lax.fori_loop(0, blocks, forward, 0)
         lax.fori_loop(0, blocks, backward, 0)
 
+    @pl.when(helps)
+    def _():
+        lax.fori_loop(0, blocks, forward_rows, 0)
+        lax.fori_loop(0, blocks, gradient, 0)
+
     for j in reversed(range(slots)):
         for n in range(2):
             wait_bytes(g_recv.at[n, j], g_rsem.at[n, j])
@@ -319,22 +415,34 @@
 
     most = pl.ds(0, dps - 1)
     for n in range(2):
-        mine = place == n * share
-
-        @pl.when(jnp.logical_not(mine))
+
+        @pl.when(place != n * share)
         def _():
             wait_bytes(k_ref.at[n], k_ssem.at[n])
+
+        @pl.when(place != n * share + 1)
+        def _():
             for j in range(slots):
-                wait_bytes(g_recv.at[n, j], w_ssem.at[n, j])
-
-        @pl.when(mine)
+                wait_bytes(g_recv.at[n, j, pl.ds(0, half)], w_ssem.at[n, j])
+
+        @pl.when(place == n * share + 1)
         def _():
             for j in range(slots):
-                wait_bytes(g_recv.at[n, j, most], w_ssem.at[n, j])
+                wait_bytes(g_recv.at[n, j, pl.ds(0, half - 1)], w_ssem.at[n, j])
 
     @pl.when(works)
     def _():
         def drain(b, carry):
+            hand_h(b).wait_send()
+            hand_up(b).wait_send()
+            return carry
+
+        lax.fori_loop(0, blocks, drain, 0)
+
+    @pl.when(helps)
+    def _():
+        def drain(b, carry):
+            wait_bytes(w_full.at[b], f_ssem.at[b])
             own = b // slots == place
 
             @pl.when(own)
@@ -368,14 +476,20 @@
             pltpu.VMEM((blocks, cells, width), bf),
             pltpu.VMEM((blocks, cells // SUB, SUB, width), f32),
             pltpu.VMEM((segments, slots, taps.shape[2], width), bf),
-            pltpu.VMEM((blocks, dps, rows, width), bf),
+            pltpu.VMEM((blocks, dps // 2, 2, rows, width), bf),
             pltpu.VMEM((blocks, dps, rows, width), bf),
             pltpu.VMEM((2, slots, dps, rows, width), bf),
             pltpu.VMEM((4, cells // SUB, SUB, width), f32),
             pltpu.VMEM((blocks, 25, SUB, width), f32),
+            pltpu.VMEM((blocks, dps // 2, rows, width), bf),
+            pltpu.VMEM((blocks, cells, width), bf),
+            pltpu.VMEM((blocks, cells, width), bf),
             pltpu.VMEM((width, width), f32),
-            dma((2,)), dma((segments,)),
-            dma((2, slots)), dma((blocks,)), dma((blocks,)), dma((2, slots)),
+            dma((2,)), dma((segments,)), dma((2, slots)),
+        ]
+        + [dma((blocks,))] * 8
+        + [
+            dma((2, slots)),
         ],
         compiler_params=pltpu.CompilerParams(
             collective_id=0, has_side_effects=True, vmem_limit_bytes=52 * 1024 * 1024
@@ -400,25 +514,12 @@
     slots = kernels.shape[0]
     side = images.shape[1]
     total_rows = images.shape[0] * side * side * dps
-    taps, w_rows, w_live, m_rows, v_rows = pick(
-        picks, section_sizes, kernels, weights, first_moment, second_moment
-    )
+    taps, w_live = pick(picks, section_sizes, kernels, weights)
     summed = train(
         segments, dps, side, to_cells(images[0]), to_cells(cotangent[:, 0]), taps, w_live
     )
-    same = (picks[0] == picks[1])[None, :, None, None]
-    live = (jnp.arange(slots) < section_sizes[0])[None, :, None, None]
-    grad = (summed + jnp.where(same, summed[::-1], 0.0)) / total_rows
-    next_m = first_decay * m_rows + (1.0 - first_decay) * grad
-    next_v = second_decay * v_rows + (1.0 - second_decay) * grad * grad
-    next_w = (
-        w_rows.astype(jnp.float32)
-        - learn_rate * (next_m / first_bias) / (jnp.sqrt(next_v / second_bias) + adam_epsilon)
-    ).astype(jnp.bfloat16)
-    return (
-        jnp.where(live, next_w, w_rows),
-        jnp.where(live, next_m, m_rows),
-        jnp.where(live, next_v, v_rows),
+    return adam(
+        total_rows, picks, section_sizes, summed, weights, first_moment, second_moment
     )
 
 

time: 80.7 us -> 75.9 us (0.941)
  other arithmetic: 3.23 us -> 0 us
  local copies, waits for them, and re-layouts: 5.43 us -> 4.59 us
    pallas_call x1, Pallas kernels: 67.3 us -> 63.4 us  [train(): pl.pallas_call(functools.partial(train_kernel, segments, dps, side), out_...]
    select_n x2 -> x0, other arithmetic: 3.22 us -> none  [the longest x1 2.21 us: body(): jnp.where(live, next_w, w_rows)]
    pallas_call x0 -> x1, Pallas kernels: none -> 3.18 us  [adam(): pl.pallas_call(functools.partial(adam_kernel, total_rows), out_shape=tupl...]
    unnamed x15 -> x6, local copies, waits for them, and re-layouts: 5.22 us -> 2.5 us
    another operation x2, local copies, waits for them, and re-layouts: 0.11 us -> 1.99 us  [to_cells(): split = field.reshape(lead + (side // 2, 2, side, width))]
where the time goes in v2:
time: 75.9 us; the launch traced here: 75.6 us
  Pallas kernels  69.6 us (92%)
  local copies, waits for them, and re-layouts  4.59 us (6%)
  between operations  1.33 us (2%)
    pallas_call x1, Pallas kernels, train(): pl.pallas_call(functools.partial(train_kernel, segments, dps, side), out_...  63.4 us
    pallas_call x1, Pallas kernels, adam(): pl.pallas_call(functools.partial(adam_kernel, total_rows), out_shape=tupl...  3.18 us
    pallas_call x1, Pallas kernels, pick(): pl.pallas_call(pick_kernel, out_shape=(shape((2, slots, taps, width), jnp...  3 us
    unnamed x6, local copies, waits for them, and re-layouts  2.5 us
    another operation x2, local copies, waits for them, and re-layouts, to_cells(): split = field.reshape(lead + (side // 2, 2, side, width))  1.99 us

profile of v2, /device:TPU:0, one launch (start us, length us, event | category | flops | bytes accessed | tf_op | source)
XLA Modules:
  0.0 75.6 jit_solution(14373623226536219012)
XLA Ops:
  1.3 3.0 %pick_rows.1 = (bf16[2,2,25,384]{3,2,1,0:T(8,128)(2,1)}, bf16[2,2,48,384]{3,2,1,0:T(8,128)(2,1)}) custom-call(s32[2,2]{1,0:T(2,128)} %picks_ref.3, s32[1]{0:T(128)S(6)} %copy.17.size_ref, bf16[2,25,48,384]{3,2,1,0:T(8,128)(2,1)} %bitcast.13, bf16[2,48,48,384]{3,2,1,0:T(8,128)(2,1)} %w_hbm.3), custom_call_target="tpu_custom_call" | custom-call | tf_op jit(solution)/shard_map/pick_rows/pallas_call | solution.py:61
  4.3 1.0 %copy.15 = bf16[2,7,2,14,384]{4,1,3,2,0:T(8,128)(2,1)S(1)} copy(bf16[2,7,2,14,384]{4,0,3,2,1:T(2,128)(2,1)} %bitcast.16) | data formatting | bytes 602112 | tf_op jit(solution)/shard_map/reshape;squeeze | solution.py:505
  5.3 0.1 pad.9
  5.4 1.0 %copy.16 = bf16[7,2,14,384]{3,0,2,1:T(8,128)(2,1)S(1)} copy(bf16[7,2,14,384]{3,2,1,0:T(8,128)(2,1)} %bitcast.17) | data formatting | bytes 301056 | tf_op jit(solution)/shard_map/reshape;squeeze | solution.py:505
  6.4 0.0 copy-start.1
  6.4 0.9 %copy-done.1 = bf16[2,2,48,384]{3,2,1,0:T(8,128)(2,1)S(1)} copy-done((bf16[2,2,48,384]{3,2,1,0:T(8,128)(2,1)S(1)}, bf16[2,2,48,384]{3,2,1,0:T(8,128)(2,1)}, u32[]{:S(2)}) %copy-start.1) | copy-done | bytes 147480
  7.3 0.0 copy-start.2
  7.3 0.9 %copy-done.2 = bf16[2,2,25,384]{3,2,1,0:T(8,128)(2,1)S(1)} copy-done((bf16[2,2,25,384]{3,2,1,0:T(8,128)(2,1)S(1)}, bf16[2,2,25,384]{3,2,1,0:T(8,128)(2,1)}, u32[]{:S(2)}) %copy-start.2) | copy-done | bytes 76824
  8.2 63.4 %train_window.1.g_ref = f32[2,2,48,384]{3,2,1,0:T(8,128)S(1)} custom-call(bf16[224,384]{1,0:T(8,128)(2,1)S(1)} %bitcast.12, bf16[2,224,384]{2,1,0:T(8,128)(2,1)S(1)} %bitcast.11, bf16[2,2,25,384]{3,2,1,0:T(8,128)(2,1)S(1)} %copy-done.2, bf16[2,2,48,384]{3,2,1,0:T(8,128)(2,1)S(1)} %copy-done.1), custom_call_target="tpu_custom_call" | custom-call | tf_op jit(solution)/shard_map/train_window/pallas_call | solution.py:468
  71.7 0.0 copy-start
  71.7 0.7 copy-done
  72.4 3.2 %adam_rows.1 = (bf16[2,2,48,384]{3,2,1,0:T(8,128)(2,1)}, f32[2,2,48,384]{3,2,1,0:T(8,128)}, f32[2,2,48,384]{3,2,1,0:T(8,128)}) custom-call(s32[2,2]{1,0:T(2,128)} %picks_ref.3, s32[1]{0:T(128)S(6)} %copy.17.size_ref, f32[2,2,48,384]{3,2,1,0:T(8,128)} %copy-done, bf16[2,48,48,384]{3,2,1,0:T(8,128)(2,1)} %w_hbm.3, f32[2,48,48,384]{3,2,1,0:T(8,128)} %m_hbm.1, ...), custom_call_target="tpu_custom_call" | custom-call | tf_op jit(solution)/shard_map/adam_rows/pallas_call | solution.py:117
  (1 shorter events, 0.0 us)
Async XLA Ops:
  6.4 0.9 %copy-start.1 = (bf16[2,2,48,384]{3,2,1,0:T(8,128)(2,1)S(1)}, bf16[2,2,48,384]{3,2,1,0:T(8,128)(2,1)}, u32[]{:S(2)}) copy-start(bf16[2,2,48,384]{3,2,1,0:T(8,128)(2,1)} %get-tuple-element.6.w_ref) | copy-start | bytes 442372
  7.3 0.9 %copy-start.2 = (bf16[2,2,25,384]{3,2,1,0:T(8,128)(2,1)S(1)}, bf16[2,2,25,384]{3,2,1,0:T(8,128)(2,1)}, u32[]{:S(2)}) copy-start(bf16[2,2,25,384]{3,2,1,0:T(8,128)(2,1)} %get-tuple-element.5.k_ref) | copy-start | bytes 230404
  71.7 0.7 copy-start

commit v3 on v2

--- a/solution.py
+++ b/solution.py
@@ -134,29 +134,27 @@
 
 def conv_columns(shifted, taps, side, lanes, emit):
     weights = [taps(t) for t in range(25)]
-    loaded = {}
-
-    def cell(sh, r, q):
-        if (sh, r, q) not in loaded:
-            loaded[sh, r, q] = shifted[sh + 1, r * side + q, :, lanes]
-        return loaded[sh, r, q]
-
+    totals = {}
     for q in range(side):
-        for r in range(2):
-            parts = []
-            for e in range(-2, 3):
-                if not 0 <= q + e < side:
-                    continue
+        column = {
+            (sh, r): shifted[sh + 1, r * side + q, :, lanes]
+            for sh in (-1, 0, 1)
+            for r in range(2)
+        }
+        for e in range(2, -3, -1):
+            out = q - e
+            if not 0 <= out < side:
+                continue
+            for r in range(2):
                 part = None
                 for a in range(-2, 3):
-                    sh, rr = (r + a) // 2, (r + a) % 2
-                    term = weights[(a + 2) * 5 + e + 2] * cell(sh, rr, q + e)
+                    term = weights[(a + 2) * 5 + e + 2] * column[(r + a) // 2, (r + a) % 2]
                     part = term if part is None else part + term
-                parts.append(part)
-            total = parts[0]
-            for part in parts[1:]:
-                total = total + part
-            emit(r, q, total)
+                totals[r, out] = totals[r, out] + part if (r, out) in totals else part
+        for out in range(side) if q == side - 1 else (q - 2,):
+            for r in range(2):
+                if (r, out) in totals:
+                    emit(r, out, totals.pop((r, out)))
 
 
 def train_kernel(
@@ -164,8 +162,9 @@
     image_ref, cot_ref, k_ref, w_ref,
     g_out,
     x_buf, up_buf, h_buf, act_buf, k_full, w_full, g_send, g_recv, shifted, taps_wide,
-    stage, h_in, up_in, joined,
-    k_ssem, k_rsem, w_ssem, s_rsem, f_ssem, w_rsem, h_ssem, h_rsem, u_ssem, u_rsem, g_ssem, g_rsem,
+    stage, h_in, up_in, pair_in, pair_sum, joined,
+    k_ssem, k_rsem, w_ssem, s_rsem, f_ssem, w_rsem, h_ssem, h_rsem, u_ssem, u_rsem, p_ssem, p_rsem,
+    g_ssem, g_rsem,
 ):
     place = lax.axis_index("segment")
     me = lax.axis_index("dp")
@@ -259,11 +258,13 @@
 
     def store_grad(b, grad):
         if aligned:
-            g_send[b] = grad.astype(jnp.bfloat16).reshape(dps, rows, width)
+            pieces = grad.astype(jnp.bfloat16).reshape(half, 2, rows, width)
+            g_send[b, 0] = pieces[:, 0]
+            g_send[b, 1] = pieces[:, 1]
         else:
             joined[...] = grad
             for k in range(dps):
-                g_send[b, k] = joined[k * rows : (k + 1) * rows].astype(jnp.bfloat16)
+                g_send[b, k % 2, k // 2] = joined[k * rows : (k + 1) * rows].astype(jnp.bfloat16)
 
     def forward_rows(b, carry):
         wait_bytes(stage.at[b], s_rsem.at[b])
@@ -332,6 +333,36 @@
 
         return carry
 
+    def pair(b):
+        return pltpu.make_async_remote_copy(
+            src_ref=g_send.at[b, 1 - low],
+            dst_ref=pair_in.at[b],
+            send_sem=p_ssem.at[b],
+            recv_sem=p_rsem.at[b],
+            device_id={"dp": (me // 2) * 2 + 1 - low},
+            device_id_type=MESH,
+        )
+
+    def scatter(b):
+        pair(b).wait_recv()
+        pair_sum[b] = (
+            g_send[b, low].astype(jnp.float32) + pair_in[b].astype(jnp.float32)
+        ).astype(jnp.bfloat16)
+
+        def send_grad(k, carry):
+            hi = lax.rem(me // 2 + k, half)
+            send(
+                pair_sum.at[b, hi],
+                g_recv.at[net, lax.rem(b, slots), me // 2],
+                g_ssem.at[b],
+                g_rsem.at[net, lax.rem(b, slots)],
+                b // slots,
+                hi * 2 + low,
+            )
+            return carry
+
+        lax.fori_loop(0, half, send_grad, 0)
+
     def gradient(i, carry):
         b = blocks - 1 - i
         hand_h(b).wait_recv()
@@ -343,20 +374,12 @@
             preferred_element_type=jnp.float32,
         )
         store_grad(b, grad)
-
-        def send_grad(k, carry):
-            owner = lax.rem(me + k, dps)
-            send(
-                g_send.at[b, owner],
-                g_recv.at[net, lax.rem(b, slots), me],
-                g_ssem.at[b],
-                g_rsem.at[net, lax.rem(b, slots)],
-                b // slots,
-                owner,
-            )
-            return carry
-
-        lax.fori_loop(0, dps, send_grad, 0)
+        pair(b).start()
+
+        @pl.when(i > 0)
+        def _():
+            scatter(b + 1)
+
         return carry
 
     def backward(i, carry):
@@ -403,6 +426,7 @@
     def _():
         lax.fori_loop(0, blocks, forward_rows, 0)
         lax.fori_loop(0, blocks, gradient, 0)
+        scatter(0)
 
     for j in reversed(range(slots)):
         for n in range(2):
@@ -411,9 +435,9 @@
             def add(d, total):
                 return total + g_recv[n, j, d].astype(jnp.float32)
 
-            g_out[n, j] = lax.fori_loop(0, dps, add, jnp.zeros((rows, width), jnp.float32))
-
-    most = pl.ds(0, dps - 1)
+            g_out[n, j] = lax.fori_loop(0, half, add, jnp.zeros((rows, width), jnp.float32))
+
+    most = pl.ds(0, half - 1)
     for n in range(2):
 
         @pl.when(place != n * share)
@@ -423,12 +447,12 @@
         @pl.when(place != n * share + 1)
         def _():
             for j in range(slots):
-                wait_bytes(g_recv.at[n, j, pl.ds(0, half)], w_ssem.at[n, j])
+                wait_bytes(g_recv.at[n, j], w_ssem.at[n, j])
 
         @pl.when(place == n * share + 1)
         def _():
             for j in range(slots):
-                wait_bytes(g_recv.at[n, j, pl.ds(0, half - 1)], w_ssem.at[n, j])
+                wait_bytes(g_recv.at[n, j, most], w_ssem.at[n, j])
 
     @pl.when(works)
     def _():
@@ -443,15 +467,16 @@
     def _():
         def drain(b, carry):
             wait_bytes(w_full.at[b], f_ssem.at[b])
+            pair(b).wait_send()
             own = b // slots == place
 
             @pl.when(own)
             def _():
-                wait_bytes(g_send.at[b, most], g_ssem.at[b])
+                wait_bytes(pair_sum.at[b, most], g_ssem.at[b])
 
             @pl.when(jnp.logical_not(own))
             def _():
-                wait_bytes(g_send.at[b], g_ssem.at[b])
+                wait_bytes(pair_sum.at[b], g_ssem.at[b])
 
             return carry
 
@@ -465,6 +490,9 @@
     vmem = pl.BlockSpec(memory_space=pltpu.VMEM)
     dma = pltpu.SemaphoreType.DMA
     bf, f32 = jnp.bfloat16, jnp.float32
+    pieces = blocks * dps * (rows + -rows % 16) * width * 2
+    limit = 4 * pieces + blocks * (7 * cells + 32 * SUB) * width * 4 + (4 << 20)
+    limit = min(limit, 56 << 20)
     return pl.pallas_call(
         functools.partial(train_kernel, segments, dps, side),
         out_shape=jax.ShapeDtypeStruct((2, slots, rows, width), f32),
@@ -477,22 +505,24 @@
             pltpu.VMEM((blocks, cells // SUB, SUB, width), f32),
             pltpu.VMEM((segments, slots, taps.shape[2], width), bf),
             pltpu.VMEM((blocks, dps // 2, 2, rows, width), bf),
-            pltpu.VMEM((blocks, dps, rows, width), bf),
-            pltpu.VMEM((2, slots, dps, rows, width), bf),
+            pltpu.VMEM((blocks, 2, dps // 2, rows, width), bf),
+            pltpu.VMEM((2, slots, dps // 2, rows, width), bf),
             pltpu.VMEM((4, cells // SUB, SUB, width), f32),
             pltpu.VMEM((blocks, 25, SUB, width), f32),
             pltpu.VMEM((blocks, dps // 2, rows, width), bf),
             pltpu.VMEM((blocks, cells, width), bf),
             pltpu.VMEM((blocks, cells, width), bf),
+            pltpu.VMEM((blocks, dps // 2, rows, width), bf),
+            pltpu.VMEM((blocks, dps // 2, rows, width), bf),
             pltpu.VMEM((width, width), f32),
             dma((2,)), dma((segments,)), dma((2, slots)),
         ]
-        + [dma((blocks,))] * 8
+        + [dma((blocks,))] * 10
         + [
             dma((2, slots)),
         ],
         compiler_params=pltpu.CompilerParams(
-            collective_id=0, has_side_effects=True, vmem_limit_bytes=52 * 1024 * 1024
+            collective_id=0, has_side_effects=True, vmem_limit_bytes=limit
         ),
         name="train_window",
     )(image, cot, taps, rows_live)

time: 75.9 us -> 69.8 us (0.920)
  Pallas kernels: 69.6 us -> 63.5 us
    pallas_call x1, Pallas kernels: 63.4 us -> 57.3 us  [train(): pl.pallas_call(functools.partial(train_kernel, segments, dps, side), out_...]
where the time goes in v3:
time: 69.8 us; the launch traced here: 69.4 us
  Pallas kernels  63.5 us (91%)
  local copies, waits for them, and re-layouts  4.59 us (7%)
  between operations  1.33 us (2%)
    pallas_call x1, Pallas kernels, train(): pl.pallas_call(functools.partial(train_kernel, segments, dps, side), out_...  57.3 us
    pallas_call x1, Pallas kernels, adam(): pl.pallas_call(functools.partial(adam_kernel, total_rows), out_shape=tupl...  3.18 us
    pallas_call x1, Pallas kernels, pick(): pl.pallas_call(pick_kernel, out_shape=(shape((2, slots, taps, width), jnp...  3 us
    unnamed x6, local copies, waits for them, and re-layouts  2.5 us
    another operation x2, local copies, waits for them, and re-layouts, to_cells(): split = field.reshape(lead + (side // 2, 2, side, width))  1.99 us

profile of v3, /device:TPU:0, one launch (start us, length us, event | category | flops | bytes accessed | tf_op | source)
XLA Modules:
  0.0 69.4 jit_solution(5052541292566395127)
XLA Ops:
  1.3 3.0 %pick_rows.1 = (bf16[2,2,25,384]{3,2,1,0:T(8,128)(2,1)}, bf16[2,2,48,384]{3,2,1,0:T(8,128)(2,1)}) custom-call(s32[2,2]{1,0:T(2,128)} %picks_ref.3, s32[1]{0:T(128)S(6)} %copy.17.size_ref, bf16[2,25,48,384]{3,2,1,0:T(8,128)(2,1)} %bitcast.13, bf16[2,48,48,384]{3,2,1,0:T(8,128)(2,1)} %w_hbm.3), custom_call_target="tpu_custom_call" | custom-call | tf_op jit(solution)/shard_map/pick_rows/pallas_call | solution.py:61
  4.3 1.0 %copy.15 = bf16[2,7,2,14,384]{4,1,3,2,0:T(8,128)(2,1)S(1)} copy(bf16[2,7,2,14,384]{4,0,3,2,1:T(2,128)(2,1)} %bitcast.16) | data formatting | bytes 602112 | tf_op jit(solution)/shard_map/reshape;squeeze | solution.py:535
  5.3 0.1 pad.9
  5.4 1.0 %copy.16 = bf16[7,2,14,384]{3,0,2,1:T(8,128)(2,1)S(1)} copy(bf16[7,2,14,384]{3,2,1,0:T(8,128)(2,1)} %bitcast.17) | data formatting | bytes 301056 | tf_op jit(solution)/shard_map/reshape;squeeze | solution.py:535
  6.4 0.0 copy-start.1
  6.4 0.9 %copy-done.1 = bf16[2,2,48,384]{3,2,1,0:T(8,128)(2,1)S(1)} copy-done((bf16[2,2,48,384]{3,2,1,0:T(8,128)(2,1)S(1)}, bf16[2,2,48,384]{3,2,1,0:T(8,128)(2,1)}, u32[]{:S(2)}) %copy-start.1) | copy-done | bytes 147480
  7.3 0.0 copy-start.2
  7.3 0.9 %copy-done.2 = bf16[2,2,25,384]{3,2,1,0:T(8,128)(2,1)S(1)} copy-done((bf16[2,2,25,384]{3,2,1,0:T(8,128)(2,1)S(1)}, bf16[2,2,25,384]{3,2,1,0:T(8,128)(2,1)}, u32[]{:S(2)}) %copy-start.2) | copy-done | bytes 76824
  8.2 57.3 %train_window.1.g_ref = f32[2,2,48,384]{3,2,1,0:T(8,128)S(1)} custom-call(bf16[224,384]{1,0:T(8,128)(2,1)S(1)} %bitcast.12, bf16[2,224,384]{2,1,0:T(8,128)(2,1)S(1)} %bitcast.11, bf16[2,2,25,384]{3,2,1,0:T(8,128)(2,1)S(1)} %copy-done.2, bf16[2,2,48,384]{3,2,1,0:T(8,128)(2,1)S(1)} %copy-done.1), custom_call_target="tpu_custom_call" | custom-call | tf_op jit(solution)/shard_map/train_window/pallas_call | solution.py:496
  65.5 0.0 copy-start
  65.5 0.7 %copy-done = f32[2,2,48,384]{3,2,1,0:T(8,128)} copy-done((f32[2,2,48,384]{3,2,1,0:T(8,128)}, f32[2,2,48,384]{3,2,1,0:T(8,128)S(1)}, u32[]{:S(2)}) %copy-start) | copy-done | bytes 294936
  66.2 3.2 %adam_rows.1 = (bf16[2,2,48,384]{3,2,1,0:T(8,128)(2,1)}, f32[2,2,48,384]{3,2,1,0:T(8,128)}, f32[2,2,48,384]{3,2,1,0:T(8,128)}) custom-call(s32[2,2]{1,0:T(2,128)} %picks_ref.3, s32[1]{0:T(128)S(6)} %copy.17.size_ref, f32[2,2,48,384]{3,2,1,0:T(8,128)} %copy-done, bf16[2,48,48,384]{3,2,1,0:T(8,128)(2,1)} %w_hbm.3, f32[2,48,48,384]{3,2,1,0:T(8,128)} %m_hbm.1, ...), custom_call_target="tpu_custom_call" | custom-call | tf_op jit(solution)/shard_map/adam_rows/pallas_call | solution.py:117
  (1 shorter events, 0.0 us)
Async XLA Ops:
  6.4 0.9 %copy-start.1 = (bf16[2,2,48,384]{3,2,1,0:T(8,128)(2,1)S(1)}, bf16[2,2,48,384]{3,2,1,0:T(8,128)(2,1)}, u32[]{:S(2)}) copy-start(bf16[2,2,48,384]{3,2,1,0:T(8,128)(2,1)} %get-tuple-element.6.w_ref) | copy-start | bytes 442372
  7.3 0.9 %copy-start.2 = (bf16[2,2,25,384]{3,2,1,0:T(8,128)(2,1)S(1)}, bf16[2,2,25,384]{3,2,1,0:T(8,128)(2,1)}, u32[]{:S(2)}) copy-start(bf16[2,2,25,384]{3,2,1,0:T(8,128)(2,1)} %get-tuple-element.5.k_ref) | copy-start | bytes 230404
  65.5 0.7 %copy-start = (f32[2,2,48,384]{3,2,1,0:T(8,128)}, f32[2,2,48,384]{3,2,1,0:T(8,128)S(1)}, u32[]{:S(2)}) copy-start(f32[2,2,48,384]{3,2,1,0:T(8,128)S(1)} %train_window.1.g_ref) | copy-start | bytes 884740

commit v4 on v3

--- a/solution.py
+++ b/solution.py
@@ -126,42 +126,38 @@
     )(picks, sizes, summed, weights, first, second)
 
 
-def put_shifts(shifted, value, lanes):
-    shifted[1, :, :, lanes] = value
-    shifted[0, :, :, lanes] = pltpu.roll(value, 1, 1)
-    shifted[2, :, :, lanes] = pltpu.roll(value, SUB - 1, 1)
-
-
-def conv_columns(shifted, taps, side, lanes, emit):
+def put_columns(cols, value, lanes):
+    moved = {0: value, -1: pltpu.roll(value, 1, 2), 1: pltpu.roll(value, SUB - 1, 2)}
+    for a in range(-2, 3):
+        halves = [moved[(r + a) // 2][:, (r + a) % 2] for r in range(2)]
+        cols[a + 2, :, :, lanes] = jnp.concatenate(halves, axis=1).astype(jnp.bfloat16)
+
+
+def conv_columns(cols, taps, side, lanes, emit):
     weights = [taps(t) for t in range(25)]
     totals = {}
     for q in range(side):
-        column = {
-            (sh, r): shifted[sh + 1, r * side + q, :, lanes]
-            for sh in (-1, 0, 1)
-            for r in range(2)
-        }
+        column = [cols[a, q, :, lanes] for a in range(5)]
         for e in range(2, -3, -1):
             out = q - e
             if not 0 <= out < side:
                 continue
-            for r in range(2):
-                part = None
-                for a in range(-2, 3):
-                    term = weights[(a + 2) * 5 + e + 2] * column[(r + a) // 2, (r + a) % 2]
-                    part = term if part is None else part + term
-                totals[r, out] = totals[r, out] + part if (r, out) in totals else part
+            part = None
+            for a in range(5):
+                term = weights[a * 5 + e + 2] * column[a]
+                part = term if part is None else part + term
+            part = part.astype(jnp.float32)
+            totals[out] = totals[out] + part if out in totals else part
         for out in range(side) if q == side - 1 else (q - 2,):
-            for r in range(2):
-                if (r, out) in totals:
-                    emit(r, out, totals.pop((r, out)))
+            if out in totals:
+                emit(out, totals.pop(out))
 
 
 def train_kernel(
     segments, dps, side,
     image_ref, cot_ref, k_ref, w_ref,
     g_out,
-    x_buf, up_buf, h_buf, act_buf, k_full, w_full, g_send, g_recv, shifted, taps_wide,
+    x_buf, up_buf, h_buf, act_buf, k_full, w_full, g_send, g_recv, cols, back_buf, taps_wide,
     stage, h_in, up_in, pair_in, pair_sum, joined,
     k_ssem, k_rsem, w_ssem, s_rsem, f_ssem, w_rsem, h_ssem, h_rsem, u_ssem, u_rsem, p_ssem, p_rsem,
     g_ssem, g_rsem,
@@ -244,7 +240,11 @@
 
         lax.fori_loop(0, half, send_rows, 0)
 
-    inside = lax.broadcasted_iota(jnp.int32, (SUB, LANES), 0) < side // 2
+    row = lax.broadcasted_iota(jnp.int32, (2 * SUB, LANES), 0)
+    inside = jnp.where(row < SUB, row, row - SUB) < side // 2
+
+    def column_of(q):
+        return pl.ds(q * 2 * SUB, 2 * SUB)
 
     def lane_slice(ct):
         return pl.ds(pl.multiple_of(ct * LANES, LANES), LANES)
@@ -300,26 +300,24 @@
         for j in range(slots):
             for t in range(25):
                 taps_wide[s * slots + j, t] = jnp.broadcast_to(
-                    k_full[s, j, t : t + 1, :].astype(jnp.float32), (SUB, width)
-                )
+                    k_full[s, j, t : t + 1, :].astype(jnp.float32), (2 * SUB, width)
+                ).astype(jnp.bfloat16)
         return carry
 
     def forward(b, carry):
         def tile(ct, carry):
             lanes = lane_slice(ct)
-            value = x_buf[b, :, lanes].astype(jnp.float32).reshape(2 * side, SUB, LANES)
-            put_shifts(shifted, value, lanes)
-
-            def emit(r, q, u):
+            value = x_buf[b, :, lanes].astype(jnp.float32).reshape(side, 2, SUB, LANES)
+            put_columns(cols, value, lanes)
+
+            def emit(q, u):
                 s = 0.5 * jnp.tanh(0.5 * u) + 0.5
-                at = r * side + q
-                act_buf[b, at, :, lanes] = jnp.where(inside, s * (1.0 + u * (1.0 - s)), 0.0)
-                shifted[3, at, :, lanes] = jnp.where(inside, u * s, 0.0)
-
-            conv_columns(shifted, lambda t: taps_wide[b, t, :, lanes], side, lanes, emit)
-            h_buf[b, :, lanes] = (
-                shifted[3, :, :, lanes].reshape(cells, LANES).astype(jnp.bfloat16)
-            )
+                act_buf[b, q, :, lanes] = jnp.where(inside, s * (1.0 + u * (1.0 - s)), 0.0)
+                h_buf[b, column_of(q), lanes] = jnp.where(inside, u * s, 0.0).astype(
+                    jnp.bfloat16
+                )
+
+            conv_columns(cols, lambda t: taps_wide[b, t, :, lanes], side, lanes, emit)
             return carry
 
         lax.fori_loop(0, tiles, tile, 0)
@@ -394,22 +392,20 @@
                 (((1,), (1,)), ((), ())),
                 preferred_element_type=jnp.float32,
             )
-            shifted[3] = back.reshape(2 * side, SUB, width)
+            back_buf[...] = back.reshape(side, 2 * SUB, width)
 
             def tile(ct, carry):
                 lanes = lane_slice(ct)
-                put_shifts(shifted, shifted[3, :, :, lanes] * act_buf[b, :, :, lanes], lanes)
-
-                def emit(r, q, total):
-                    shifted[3, r * side + q, :, lanes] = jnp.where(inside, total, 0.0)
-
-                conv_columns(
-                    shifted, lambda t: taps_wide[b, 24 - t, :, lanes], side, lanes, emit
-                )
-                up_buf[b, :, lanes] = (
-                    up_buf[b + 1, :, lanes].astype(jnp.float32)
-                    + shifted[3, :, :, lanes].reshape(cells, LANES)
-                ).astype(jnp.bfloat16)
+                value = back_buf[:, :, lanes] * act_buf[b, :, :, lanes]
+                put_columns(cols, value.reshape(side, 2, SUB, LANES), lanes)
+
+                def emit(q, total):
+                    up_buf[b, column_of(q), lanes] = (
+                        up_buf[b + 1, column_of(q), lanes].astype(jnp.float32)
+                        + jnp.where(inside, total, 0.0)
+                    ).astype(jnp.bfloat16)
+
+                conv_columns(cols, lambda t: taps_wide[b, 24 - t, :, lanes], side, lanes, emit)
                 return carry
 
             lax.fori_loop(0, tiles, tile, 0)
@@ -496,19 +492,20 @@
     return pl.pallas_call(
         functools.partial(train_kernel, segments, dps, side),
         out_shape=jax.ShapeDtypeStruct((2, slots, rows, width), f32),
-        in_specs=[vmem] * 4,
+        in_specs=[vmem, vmem, pl.BlockSpec(memory_space=pl.ANY), pl.BlockSpec(memory_space=pl.ANY)],
         out_specs=vmem,
         scratch_shapes=[
             pltpu.VMEM((blocks, cells, width), bf),
             pltpu.VMEM((blocks + 1, cells, width), bf),
             pltpu.VMEM((blocks, cells, width), bf),
-            pltpu.VMEM((blocks, cells // SUB, SUB, width), f32),
+            pltpu.VMEM((blocks, side, 2 * SUB, width), f32),
             pltpu.VMEM((segments, slots, taps.shape[2], width), bf),
             pltpu.VMEM((blocks, dps // 2, 2, rows, width), bf),
             pltpu.VMEM((blocks, 2, dps // 2, rows, width), bf),
             pltpu.VMEM((2, slots, dps // 2, rows, width), bf),
-            pltpu.VMEM((4, cells // SUB, SUB, width), f32),
-            pltpu.VMEM((blocks, 25, SUB, width), f32),
+            pltpu.VMEM((5, side, 2 * SUB, width), bf),
+            pltpu.VMEM((side, 2 * SUB, width), f32),
+            pltpu.VMEM((blocks, 25, 2 * SUB, width), bf),
             pltpu.VMEM((blocks, dps // 2, rows, width), bf),
             pltpu.VMEM((blocks, cells, width), bf),
             pltpu.VMEM((blocks, cells, width), bf),
@@ -533,7 +530,7 @@
     side, width = field.shape[-2], field.shape[-1]
     k = len(lead)
     split = field.reshape(lead + (side // 2, 2, side, width))
-    split = jnp.transpose(split, tuple(range(k)) + (k + 1, k + 2, k, k + 3))
+    split = jnp.transpose(split, tuple(range(k)) + (k + 2, k + 1, k, k + 3))
     split = jnp.pad(split, ((0, 0),) * (k + 2) + ((0, SUB - side // 2), (0, 0)))
     return split.reshape(lead + (2 * side * SUB, width))
 

time: 69.8 us -> 69.8 us (level)
  no operation moved by 1% of the time
where the time goes in v4:
time: 69.8 us; the launch traced here: 69.4 us
  Pallas kernels  63.5 us (91%)
  local copies, waits for them, and re-layouts  4.59 us (7%)
  between operations  1.33 us (2%)
    pallas_call x1, Pallas kernels, train(): pl.pallas_call(functools.partial(train_kernel, segments, dps, side), out_...  57.3 us
    pallas_call x1, Pallas kernels, adam(): pl.pallas_call(functools.partial(adam_kernel, total_rows), out_shape=tupl...  3.18 us
    pallas_call x1, Pallas kernels, pick(): pl.pallas_call(pick_kernel, out_shape=(shape((2, slots, taps, width), jnp...  3 us
    unnamed x6, local copies, waits for them, and re-layouts  2.5 us
    another operation x2, local copies, waits for them, and re-layouts, to_cells(): split = field.reshape(lead + (side // 2, 2, side, width))  1.99 us

profile of v4, /device:TPU:0, one launch (start us, length us, event | category | flops | bytes accessed | tf_op | source)
XLA Modules:
  0.0 69.4 jit_solution(15955571266488382410)
XLA Ops:
  1.3 3.0 %pick_rows.1 = (bf16[2,2,25,384]{3,2,1,0:T(8,128)(2,1)}, bf16[2,2,48,384]{3,2,1,0:T(8,128)(2,1)}) custom-call(s32[2,2]{1,0:T(2,128)} %picks_ref.3, s32[1]{0:T(128)S(6)} %copy.17.size_ref, bf16[2,25,48,384]{3,2,1,0:T(8,128)(2,1)} %bitcast.13, bf16[2,48,48,384]{3,2,1,0:T(8,128)(2,1)} %w_hbm.3), custom_call_target="tpu_custom_call" | custom-call | tf_op jit(solution)/shard_map/pick_rows/pallas_call | solution.py:61
  4.3 1.0 %copy.15 = bf16[2,7,2,14,384]{4,1,2,3,0:T(8,128)(2,1)S(1)} copy(bf16[2,7,2,14,384]{4,0,3,2,1:T(2,128)(2,1)} %bitcast.16) | data formatting | bytes 602112 | tf_op jit(solution)/shard_map/reshape;squeeze | solution.py:532
  5.3 0.1 pad.9
  5.4 1.0 %copy.16 = bf16[7,2,14,384]{3,0,1,2:T(8,128)(2,1)S(1)} copy(bf16[7,2,14,384]{3,2,1,0:T(8,128)(2,1)} %bitcast.17) | data formatting | bytes 301056 | tf_op jit(solution)/shard_map/reshape;squeeze | solution.py:532
  6.4 0.0 copy-start.1
  6.4 0.9 %copy-done.1 = bf16[2,2,48,384]{3,2,1,0:T(8,128)(2,1)S(1)} copy-done((bf16[2,2,48,384]{3,2,1,0:T(8,128)(2,1)S(1)}, bf16[2,2,48,384]{3,2,1,0:T(8,128)(2,1)}, u32[]{:S(2)}) %copy-start.1) | copy-done | bytes 147480
  7.3 0.0 copy-start.2
  7.3 0.9 %copy-done.2 = bf16[2,2,25,384]{3,2,1,0:T(8,128)(2,1)S(1)} copy-done((bf16[2,2,25,384]{3,2,1,0:T(8,128)(2,1)S(1)}, bf16[2,2,25,384]{3,2,1,0:T(8,128)(2,1)}, u32[]{:S(2)}) %copy-start.2) | copy-done | bytes 76824
  8.2 57.3 %train_window.1.g_ref = f32[2,2,48,384]{3,2,1,0:T(8,128)S(1)} custom-call(bf16[224,384]{1,0:T(8,128)(2,1)S(1)} %bitcast.12, bf16[2,224,384]{2,1,0:T(8,128)(2,1)S(1)} %bitcast.11, bf16[2,2,25,384]{3,2,1,0:T(8,128)(2,1)S(1)} %copy-done.2, bf16[2,2,48,384]{3,2,1,0:T(8,128)(2,1)S(1)} %copy-done.1), custom_call_target="tpu_custom_call" | custom-call | tf_op jit(solution)/shard_map/train_window/pallas_call | solution.py:492
  65.5 0.0 copy-start
  65.5 0.7 %copy-done = f32[2,2,48,384]{3,2,1,0:T(8,128)} copy-done((f32[2,2,48,384]{3,2,1,0:T(8,128)}, f32[2,2,48,384]{3,2,1,0:T(8,128)S(1)}, u32[]{:S(2)}) %copy-start) | copy-done | bytes 294936
  66.2 3.2 %adam_rows.1 = (bf16[2,2,48,384]{3,2,1,0:T(8,128)(2,1)}, f32[2,2,48,384]{3,2,1,0:T(8,128)}, f32[2,2,48,384]{3,2,1,0:T(8,128)}) custom-call(s32[2,2]{1,0:T(2,128)} %picks_ref.3, s32[1]{0:T(128)S(6)} %copy.17.size_ref, f32[2,2,48,384]{3,2,1,0:T(8,128)} %copy-done, bf16[2,48,48,384]{3,2,1,0:T(8,128)(2,1)} %w_hbm.3, f32[2,48,48,384]{3,2,1,0:T(8,128)} %m_hbm.1, ...), custom_call_target="tpu_custom_call" | custom-call | tf_op jit(solution)/shard_map/adam_rows/pallas_call | solution.py:117
  (1 shorter events, 0.0 us)
Async XLA Ops:
  6.4 0.9 %copy-start.1 = (bf16[2,2,48,384]{3,2,1,0:T(8,128)(2,1)S(1)}, bf16[2,2,48,384]{3,2,1,0:T(8,128)(2,1)}, u32[]{:S(2)}) copy-start(bf16[2,2,48,384]{3,2,1,0:T(8,128)(2,1)} %get-tuple-element.6.w_ref) | copy-start | bytes 442372
  7.3 0.9 %copy-start.2 = (bf16[2,2,25,384]{3,2,1,0:T(8,128)(2,1)S(1)}, bf16[2,2,25,384]{3,2,1,0:T(8,128)(2,1)}, u32[]{:S(2)}) copy-start(bf16[2,2,25,384]{3,2,1,0:T(8,128)(2,1)} %get-tuple-element.5.k_ref) | copy-start | bytes 230404
  65.5 0.7 %copy-start = (f32[2,2,48,384]{3,2,1,0:T(8,128)}, f32[2,2,48,384]{3,2,1,0:T(8,128)S(1)}, u32[]{:S(2)}) copy-start(f32[2,2,48,384]{3,2,1,0:T(8,128)S(1)} %train_window.1.g_ref) | copy-start | bytes 884740

commit v5 on v3

--- a/solution.py
+++ b/solution.py
@@ -490,13 +490,10 @@
     vmem = pl.BlockSpec(memory_space=pltpu.VMEM)
     dma = pltpu.SemaphoreType.DMA
     bf, f32 = jnp.bfloat16, jnp.float32
-    pieces = blocks * dps * (rows + -rows % 16) * width * 2
-    limit = 4 * pieces + blocks * (7 * cells + 32 * SUB) * width * 4 + (4 << 20)
-    limit = min(limit, 56 << 20)
     return pl.pallas_call(
         functools.partial(train_kernel, segments, dps, side),
         out_shape=jax.ShapeDtypeStruct((2, slots, rows, width), f32),
-        in_specs=[vmem] * 4,
+        in_specs=[vmem, vmem, pl.BlockSpec(memory_space=pl.ANY), pl.BlockSpec(memory_space=pl.ANY)],
         out_specs=vmem,
         scratch_shapes=[
             pltpu.VMEM((blocks, cells, width), bf),
@@ -522,7 +519,7 @@
             dma((2, slots)),
         ],
         compiler_params=pltpu.CompilerParams(
-            collective_id=0, has_side_effects=True, vmem_limit_bytes=limit
+            collective_id=0, has_side_effects=True, vmem_limit_bytes=58 << 20
         ),
         name="train_window",
     )(image, cot, taps, rows_live)

time: 69.8 us -> 70.6 us (1.011)
  Pallas kernels: 63.5 us -> 65.5 us
  local copies, waits for them, and re-layouts: 4.59 us -> 3.48 us
    unnamed x6 -> x0, local copies, waits for them, and re-layouts: 2.5 us -> none
    pallas_call x1, Pallas kernels: 57.3 us -> 59.3 us  [train(): pl.pallas_call(functools.partial(train_kernel, segments, dps, side), out_...]
    pad x2, local copies, waits for them, and re-layouts: 0.1 us -> 1.5 us  [to_cells(): split = jnp.pad(split, ((0, 0),) * (k + 2) + ((0, SUB - side // 2), (0, 0)))]
where the time goes in v5:
time: 70.6 us; the launch traced here: 70.3 us
  Pallas kernels  65.5 us (93%)
  local copies, waits for them, and re-layouts  3.48 us (5%)
  between operations  1.3 us (2%)
    pallas_call x1, Pallas kernels, train(): pl.pallas_call(functools.partial(train_kernel, segments, dps, side), out_...  59.3 us
    pallas_call x1, Pallas kernels, adam(): pl.pallas_call(functools.partial(adam_kernel, total_rows), out_shape=tupl...  3.19 us
    pallas_call x1, Pallas kernels, pick(): pl.pallas_call(pick_kernel, out_shape=(shape((2, slots, taps, width), jnp...  3 us
    another operation x2, local copies, waits for them, and re-layouts, to_cells(): split = field.reshape(lead + (side // 2, 2, side, width))  1.99 us
    pad x2, local copies, waits for them, and re-layouts, to_cells(): split = jnp.pad(split, ((0, 0),) * (k + 2) + ((0, SUB - side // 2), (0, 0)))  1.5 us

profile of v5, /device:TPU:0, one launch (start us, length us, event | category | flops | bytes accessed | tf_op | source)
XLA Modules:
  0.0 70.3 jit_solution(10725866746206782143)
XLA Ops:
  1.3 3.0 %pick_rows.1 = (bf16[2,2,25,384]{3,2,1,0:T(8,128)(2,1)}, bf16[2,2,48,384]{3,2,1,0:T(8,128)(2,1)}) custom-call(s32[2,2]{1,0:T(2,128)} %picks_ref.3, s32[1]{0:T(128)S(6)} %copy.17.size_ref, bf16[2,25,48,384]{3,2,1,0:T(8,128)(2,1)} %bitcast.11, bf16[2,48,48,384]{3,2,1,0:T(8,128)(2,1)} %w_hbm.3), custom_call_target="tpu_custom_call" | custom-call | tf_op jit(solution)/shard_map/pick_rows/pallas_call | solution.py:61
  4.3 1.0 %copy.15 = bf16[2,7,2,14,384]{4,1,3,2,0:T(8,128)(2,1)S(1)} copy(bf16[2,7,2,14,384]{4,0,3,2,1:T(2,128)(2,1)} %bitcast.16) | data formatting | bytes 602112 | tf_op jit(solution)/shard_map/reshape;squeeze | solution.py:532
  5.3 0.8 %pad.9 = bf16[2,2,14,8,384]{4,3,2,1,0:T(8,128)(2,1)} pad(bf16[2,2,14,7,384]{4,3,2,1,0:T(8,128)(2,1)S(1)} %bitcast.13, bf16[]{:T(256)} %constant.2.clone.1), padding=0_0x0_0x0_0x0_1x0_0 | pad | bytes 645122 | tf_op jit(solution)/shard_map/jit(_pad)/pad | solution.py:534
  6.1 1.0 %copy.16 = bf16[7,2,14,384]{3,0,2,1:T(8,128)(2,1)S(1)} copy(bf16[7,2,14,384]{3,2,1,0:T(8,128)(2,1)} %bitcast.17) | data formatting | bytes 301056 | tf_op jit(solution)/shard_map/reshape;squeeze | solution.py:532
  7.1 0.7 %pad.8 = bf16[2,14,8,384]{3,2,1,0:T(8,128)(2,1)} pad(bf16[2,14,7,384]{3,2,1,0:T(8,128)(2,1)S(1)} %bitcast.14, bf16[]{:T(256)} %constant.2.clone.1), padding=0_0x0_0x0_1x0_0 | pad | bytes 322562 | tf_op jit(solution)/shard_map/jit(_pad)/pad | solution.py:534
  7.8 59.3 %train_window.1.g_ref = f32[2,2,48,384]{3,2,1,0:T(8,128)} custom-call(bf16[224,384]{1,0:T(8,128)(2,1)} %bitcast.15, bf16[2,224,384]{2,1,0:T(8,128)(2,1)} %bitcast.12, bf16[2,2,25,384]{3,2,1,0:T(8,128)(2,1)} %get-tuple-element.5.k_ref, bf16[2,2,48,384]{3,2,1,0:T(8,128)(2,1)} %get-tuple-element.6.w_ref), custom_call_target="tpu_custom_call" | custom-call | tf_op jit(solution)/shard_map/train_window/pallas_call | solution.py:493
  67.1 3.2 %adam_rows.1 = (bf16[2,2,48,384]{3,2,1,0:T(8,128)(2,1)}, f32[2,2,48,384]{3,2,1,0:T(8,128)}, f32[2,2,48,384]{3,2,1,0:T(8,128)}) custom-call(s32[2,2]{1,0:T(2,128)} %picks_ref.3, s32[1]{0:T(128)S(6)} %copy.17.size_ref, f32[2,2,48,384]{3,2,1,0:T(8,128)} %train_window.1.g_ref, bf16[2,48,48,384]{3,2,1,0:T(8,128)(2,1)} %w_hbm.3, f32[2,48,48,384]{3,2,1,0:T(8,128)} %m_hbm.1, ...), custom_call_target="tpu_custom_call" | custom-call | tf_op jit(solution)/shard_map/adam_rows/pallas_call | solution.py:117

commit v6 on v3

--- a/solution.py
+++ b/solution.py
@@ -70,7 +70,7 @@
             pltpu.VMEM((2, slots, taps, GROUP, width), jnp.bfloat16),
             pltpu.SemaphoreType.DMA((2, 2, slots)),
         ],
-        compiler_params=pltpu.CompilerParams(vmem_limit_bytes=56 * 1024 * 1024),
+        compiler_params=pltpu.CompilerParams(vmem_limit_bytes=48 * 1024 * 1024),
         name="pick_rows",
     )(picks, sizes, jnp.transpose(kernels, (0, 2, 1, 3)), weights)
 

time: 69.8 us -> 70.8 us (1.014)
  local copies, waits for them, and re-layouts: 4.59 us -> 6.97 us
  Pallas kernels: 63.5 us -> 62.2 us
    unnamed x6 -> x8, local copies, waits for them, and re-layouts: 2.5 us -> 4.88 us
    pallas_call x1, Pallas kernels: 3 us -> 1.55 us  [pick(): pl.pallas_call(pick_kernel, out_shape=(shape((2, slots, taps, width), jnp...]
where the time goes in v6:
time: 70.8 us; the launch traced here: 70.5 us
  Pallas kernels  62.2 us (88%)
  local copies, waits for them, and re-layouts  6.97 us (10%)
  between operations  1.33 us (2%)
    pallas_call x1, Pallas kernels, train(): pl.pallas_call(functools.partial(train_kernel, segments, dps, side), out_...  57.5 us
    unnamed x8, local copies, waits for them, and re-layouts  4.88 us
    pallas_call x1, Pallas kernels, adam(): pl.pallas_call(functools.partial(adam_kernel, total_rows), out_shape=tupl...  3.18 us
    another operation x2, local copies, waits for them, and re-layouts, to_cells(): split = field.reshape(lead + (side // 2, 2, side, width))  1.99 us
    pallas_call x1, Pallas kernels, pick(): pl.pallas_call(pick_kernel, out_shape=(shape((2, slots, taps, width), jnp...  1.55 us

profile of v6, /device:TPU:0, one launch (start us, length us, event | category | flops | bytes accessed | tf_op | source)
XLA Modules:
  0.0 70.5 jit_solution(4837596283568935802)
XLA Ops:
  1.3 0.0 copy-start
  1.3 2.0 %copy-done = bf16[2,48,48,384]{3,2,1,0:T(8,128)(2,1)S(1)} copy-done((bf16[2,48,48,384]{3,2,1,0:T(8,128)(2,1)S(1)}, bf16[2,48,48,384]{3,2,1,0:T(8,128)(2,1)}, u32[]{:S(2)}) %copy-start) | copy-done | bytes 3538968
  3.3 0.0 copy-start.1
  3.3 1.5 %copy-done.1 = bf16[2,48,25,384]{3,1,2,0:T(8,128)(2,1)S(1)} copy-done((bf16[2,48,25,384]{3,1,2,0:T(8,128)(2,1)S(1)}, bf16[2,48,25,384]{3,1,2,0:T(8,128)(2,1)}, u32[]{:S(2)}) %copy-start.1) | copy-done | bytes 1843224
  4.8 0.0 copy-start.3
  4.8 0.7 copy-done.3
  5.5 1.5 %pick_rows.1 = (bf16[2,2,25,384]{3,2,1,0:T(8,128)(2,1)S(1)}, bf16[2,2,48,384]{3,2,1,0:T(8,128)(2,1)S(1)}) custom-call(s32[2,2]{1,0:T(2,128)S(1)} %copy-done.3, s32[1]{0:T(128)S(6)} %copy.17.size_ref, bf16[2,25,48,384]{3,2,1,0:T(8,128)(2,1)S(1)} %bitcast.11, bf16[2,48,48,384]{3,2,1,0:T(8,128)(2,1)S(1)} %copy-done), custom_call_target="tpu_custom_call" | custom-call | tf_op jit(solution)/shard_map/pick_rows/pallas_call | solution.py:61
  7.0 1.0 %copy.15 = bf16[2,7,2,14,384]{4,1,3,2,0:T(8,128)(2,1)S(1)} copy(bf16[2,7,2,14,384]{4,0,3,2,1:T(2,128)(2,1)} %bitcast.16) | data formatting | bytes 602112 | tf_op jit(solution)/shard_map/reshape;squeeze | solution.py:535
  8.0 0.1 pad.9
  8.1 1.0 %copy.16 = bf16[7,2,14,384]{3,0,2,1:T(8,128)(2,1)S(1)} copy(bf16[7,2,14,384]{3,2,1,0:T(8,128)(2,1)} %bitcast.17) | data formatting | bytes 301056 | tf_op jit(solution)/shard_map/reshape;squeeze | solution.py:535
  9.1 57.5 %train_window.1.g_ref = f32[2,2,48,384]{3,2,1,0:T(8,128)S(1)} custom-call(bf16[224,384]{1,0:T(8,128)(2,1)S(1)} %bitcast.13, bf16[2,224,384]{2,1,0:T(8,128)(2,1)S(1)} %bitcast.12, bf16[2,2,25,384]{3,2,1,0:T(8,128)(2,1)S(1)} %get-tuple-element.5.k_ref, bf16[2,2,48,384]{3,2,1,0:T(8,128)(2,1)S(1)} %get-tuple-element.6.w_ref), custom_call_target="tpu_custom_call" | custom-call | tf_op jit(solution)/shard_map/train_window/pallas_call | solution.py:496
  66.6 0.0 copy-start.2
  66.6 0.7 copy-done.2
  67.3 3.2 %adam_rows.1 = (bf16[2,2,48,384]{3,2,1,0:T(8,128)(2,1)}, f32[2,2,48,384]{3,2,1,0:T(8,128)}, f32[2,2,48,384]{3,2,1,0:T(8,128)}) custom-call(s32[2,2]{1,0:T(2,128)} %picks_ref.3, s32[1]{0:T(128)S(6)} %copy.17.size_ref, f32[2,2,48,384]{3,2,1,0:T(8,128)} %copy-done.2, bf16[2,48,48,384]{3,2,1,0:T(8,128)(2,1)} %w_hbm.3, f32[2,48,48,384]{3,2,1,0:T(8,128)} %m_hbm.1, ...), custom_call_target="tpu_custom_call" | custom-call | tf_op jit(solution)/shard_map/adam_rows/pallas_call | solution.py:117
  (1 shorter events, 0.0 us)
Async XLA Ops:
  1.3 2.0 %copy-start = (bf16[2,48,48,384]{3,2,1,0:T(8,128)(2,1)S(1)}, bf16[2,48,48,384]{3,2,1,0:T(8,128)(2,1)}, u32[]{:S(2)}) copy-start(bf16[2,48,48,384]{3,2,1,0:T(8,128)(2,1)} %w_hbm.3) | copy-start | bytes 10616836
  3.3 1.5 %copy-start.1 = (bf16[2,48,25,384]{3,1,2,0:T(8,128)(2,1)S(1)}, bf16[2,48,25,384]{3,1,2,0:T(8,128)(2,1)}, u32[]{:S(2)}) copy-start(bf16[2,48,25,384]{3,1,2,0:T(8,128)(2,1)} %param.12) | copy-start | bytes 5529604
  4.8 0.7 copy-start.3
  66.6 0.7 %copy-start.2 = (f32[2,2,48,384]{3,2,1,0:T(8,128)}, f32[2,2,48,384]{3,2,1,0:T(8,128)S(1)}, u32[]{:S(2)}) copy-start(f32[2,2,48,384]{3,2,1,0:T(8,128)S(1)} %train_window.1.g_ref) | copy-start | bytes 884740
